TPU v7x, 512 devices: a whole 4x8x8 slice. The times are simulated.
512 devices in a mesh: dp: 32 (over y, x), pipe: 16 (over z, core).
Axes of the slice: x: 4, y: 8, z: 8, core: 2. Of those that a mesh axis runs over, the one named last changes fastest.
Arguments:
- base_ids: int32 [32, 3, 64, 32], P('dp'), may hold values from 0 to 3
- embed_table: bfloat16 [128, 768], replicated, may hold values from -1 to 1
- segment_weights: bfloat16 [16, 768, 768], P('pipe'), may hold values from -0.21875 to 0.21875
- conv_taps: float32 [16, 3, 768], P('pipe'), may hold values from -3 to 3
- norm_gains: float32 [16, 768], P('pipe'), may hold values from 0.1 to 1.9
- cotangent: bfloat16 [32, 3, 64, 768], P('dp'), may hold values from -6 to 6
Outputs:
- weight_grads: float32 [16, 768, 768], P('pipe')
All inputs are finite; a program needn't handle non-finite values.
Results may differ from a plain program's by a relative error of at most 0.023.
Values may be sent and summed in bfloat16 or wider, within the bound.
No kernel may reach another device: no remote copies, remote signals or barrier semaphores. Data moves between devices by JAX's collectives and lax.ppermute only.
A program may use at most 64 MiB of HBM per device.

v0:
```python
import math
import jax
import jax.numpy as jnp
from jax import lax
from jax.sharding import PartitionSpec as P


def passed_along(block, axis, distance):
    devices = range(lax.axis_size(axis))
    route = [(i - distance, i) for i in devices if i - distance in devices]
    return lax.ppermute(block, axis, route)


def encode_bases(base_rows, embed_table):
    one_hot = (base_rows[:, :, None] == jnp.arange(4, dtype=jnp.int32)).astype(jnp.bfloat16)
    one_hot = one_hot.reshape(base_rows.shape[0], -1)
    return jnp.dot(one_hot, embed_table, preferred_element_type=jnp.float32).astype(jnp.bfloat16)


def section_parts(segment_input, skip_input, tap_rows, gain_row):
    inner_sum = segment_input.astype(jnp.float32) + skip_input.astype(jnp.float32)
    inv_rms = lax.rsqrt(jnp.mean(inner_sum * inner_sum, axis=-1, keepdims=True) + 1e-06)
    normed = inner_sum * inv_rms * gain_row
    padded = jnp.pad(normed, ((1, 1), (0, 0)))
    mixed = tap_rows[0] * padded[:-2] + tap_rows[1] * padded[1:-1] + tap_rows[2] * padded[2:]
    return (inner_sum, jax.nn.gelu(mixed))


def section_forward(segment_input, skip_input, weight, tap_rows, gain_row):
    inner_sum, act_full = section_parts(segment_input, skip_input, tap_rows, gain_row)
    product = jnp.dot(act_full.astype(jnp.bfloat16), weight, preferred_element_type=jnp.float32)
    return (inner_sum + product).astype(jnp.bfloat16)


def section_back(segment_input, skip_input, weight, tap_rows, gain_row, upstream):
    upstream_bf = upstream.astype(jnp.bfloat16)
    primal, pullback = jax.vjp(
        lambda first_in, second_in: section_parts(first_in, second_in, tap_rows, gain_row),
        segment_input,
        skip_input,
    )
    act_bf = primal[1].astype(jnp.bfloat16)
    weight_term = lax.dot_general(
        act_bf, upstream_bf, (((0,), (0,)), ((), ())), preferred_element_type=jnp.float32
    )
    act_grad = lax.dot_general(
        upstream_bf, weight, (((1,), (1,)), ((), ())), preferred_element_type=jnp.float32
    )
    input_grad, skip_grad = pullback((upstream, act_grad))
    return (input_grad, skip_grad, weight_term)


def store_slot(buffer, value, slot_index, is_valid):
    kept = jnp.where(is_valid, value, buffer[slot_index])
    return lax.dynamic_update_index_in_dim(buffer, kept, slot_index, 0)


def shards(base_ids, embed_table, segment_weights, conv_taps, norm_gains, cotangent):
    segments = lax.axis_size("pipe")
    quarter = segments // 4
    position = lax.axis_index("pipe")
    weight = segment_weights[0]
    tap_rows = conv_taps[0]
    gain_row = norm_gains[0]
    micro_count = base_ids.shape[1]
    row_count = base_ids.shape[2]
    channels = weight.shape[1]
    steps_total = segments + micro_count - 1
    split_step = quarter + micro_count - 1
    zero_rows = jnp.zeros((row_count, channels), jnp.bfloat16)
    zero_buffer = jnp.zeros((micro_count, row_count, channels), jnp.bfloat16)

    def forward_step(time_step, loop_state):
        arrived, stored_inputs, towers, skip_maps = loop_state
        micro_index = time_step - position
        active = (micro_index >= 0) & (micro_index < micro_count)
        slot_index = jnp.clip(micro_index, 0, micro_count - 1)

        def forward_compute(operands):
            arrived_in, skips_in = operands
            encoded = encode_bases(base_ids[0, slot_index], embed_table)
            segment_input = jnp.where(position == 0, encoded, arrived_in)
            output = section_forward(
                segment_input, skips_in[slot_index], weight, tap_rows, gain_row
            )
            return (segment_input, output)

        def forward_passthrough(operands):
            return (zero_rows, zero_rows)

        segment_input, output = lax.cond(
            active, forward_compute, forward_passthrough, (arrived, skip_maps)
        )
        stored_inputs = store_slot(stored_inputs, segment_input, slot_index, active)
        towers = store_slot(towers, output, slot_index, active)
        landed = passed_along(output, "pipe", 3 * quarter)
        source = time_step - (position - 3 * quarter)
        is_valid = (position >= 3 * quarter) & (source >= 0) & (source < micro_count)
        skip_maps = store_slot(skip_maps, landed, jnp.clip(source, 0, micro_count - 1), is_valid)
        arrived = passed_along(output, "pipe", 1)
        return (arrived, stored_inputs, towers, skip_maps)

    loop_state = (zero_rows, zero_buffer, zero_buffer, zero_buffer)
    loop_state = lax.fori_loop(0, split_step, forward_step, loop_state)
    loop_state = lax.fori_loop(split_step, steps_total, forward_step, loop_state)
    stored_inputs = loop_state[1]
    skip_maps = loop_state[3]

    def backward_step(time_step, loop_state):
        arrived, returned, skip_grads, accumulated = loop_state
        micro_index = time_step - (segments - 1 - position)
        active = (micro_index >= 0) & (micro_index < micro_count)
        slot_index = jnp.clip(micro_index, 0, micro_count - 1)

        def backward_compute(operands):
            arrived_in, returned_in, accum_in = operands
            from_next = jnp.where(
                position == segments - 1,
                cotangent[0, slot_index].astype(jnp.float32),
                arrived_in.astype(jnp.float32),
            )
            upstream = from_next + returned_in[slot_index].astype(jnp.float32)
            input_grad, skip_grad, weight_term = section_back(
                stored_inputs[slot_index],
                skip_maps[slot_index],
                weight,
                tap_rows,
                gain_row,
                upstream,
            )
            return (input_grad, skip_grad, accum_in + weight_term)

        def backward_passthrough(operands):
            return (zero_rows, zero_rows, operands[2])

        input_grad, skip_grad, accumulated = lax.cond(
            active, backward_compute, backward_passthrough, (arrived, returned, accumulated)
        )
        skip_grads = store_slot(skip_grads, skip_grad, slot_index, active)
        landed = passed_along(skip_grad, "pipe", -3 * quarter)
        source = time_step - (segments - 1 - (position + 3 * quarter))
        is_valid = (position < quarter) & (source >= 0) & (source < micro_count)
        returned = store_slot(returned, landed, jnp.clip(source, 0, micro_count - 1), is_valid)
        arrived = passed_along(input_grad, "pipe", -1)
        return (arrived, returned, skip_grads, accumulated)

    back_state = (zero_rows, zero_buffer, zero_buffer, jnp.zeros((channels, channels), jnp.float32))
    back_state = lax.fori_loop(0, split_step, backward_step, back_state)
    back_state = lax.fori_loop(split_step, steps_total, backward_step, back_state)
    total = lax.psum(back_state[3], "dp")
    factor = 1.0 / math.sqrt(lax.axis_size("dp") * micro_count * row_count)
    return (total * factor)[None]


def solution(mesh):
    return jax.shard_map(
        shards,
        mesh=mesh,
        in_specs=(
            P("dp", None, None, None),
            P(),
            P("pipe", None, None),
            P("pipe", None, None),
            P("pipe", None),
            P("dp", None, None, None),
        ),
        out_specs=P("pipe", None, None),
        check_vma=False,
    )
```

profile of v0, /device:TPU:64, one launch (start us, length us, event | category | flops | bytes accessed | tf_op | source)
XLA Modules:
  0.0 635.2 jit_solution(8572554592605807592)
XLA Ops:
  7.3 76.5 %while.84 = (s32[]{:T(128)}, bf16[64,768]{1,0:T(8,128)(2,1)S(1)}, bf16[3,64,768]{2,1,0:T(8,128)(2,1)S(1)}, bf16[3,64,768]{2,1,0:T(8,128)(2,1)S(1)}, s32[]{:T(128...) while((s32[]{:T(128)}, bf16[64,768]{1,0:T(8,128)(2,1)S(1)}, ...), condition=%wide.region_4.5_spmd, body=%wide.region_0.4_spmd.sunk | while | flops 89710664 | bytes 4455945 | solution.py:104
  9.9 10.0 %collective-permute-start.1 = (bf16[64,768]{1,0:T(8,128)(2,1)S(1)}, bf16[64,768]{1,0:T(8,128)(2,1)S(1)}, u32[]{:S(2)}, u32[]{:S(2)}) collective-permute-start(bf16[64,768]{1,0:T(8,128)(2,1)S(1)} %get-tuple-element.1675), channel_id=1, source_target_pairs={{0,12},{1,13},{2,14},{3,15},{16,28},{17,29},{18,30},{19,31},{32,44... | collective-permute-start | bytes 294920 | tf_op jit(solution)/shard_map/while/body/eval_jaxpr/ppermute | solution.py:11
  20.1 2.1 collective-permute-done.1
  24.9 6.5 %collective-permute-start.1 = (bf16[64,768]{1,0:T(8,128)(2,1)S(1)}, bf16[64,768]{1,0:T(8,128)(2,1)S(1)}, u32[]{:S(2)}, u32[]{:S(2)}) collective-permute-start(bf16[64,768]{1,0:T(8,128)(2,1)S(1)} %get-tuple-element.1675), channel_id=1, source_target_pairs={{0,12},{1,13},{2,14},{3,15},{16,28},{17,29},{18,30},{19,31},{32,44... | collective-permute-start | bytes 294920 | tf_op jit(solution)/shard_map/while/body/eval_jaxpr/ppermute | solution.py:11
  31.5 2.1 collective-permute-done.1
  35.5 6.2 conditional.8
  36.4 2.0 multiply_reduce_fusion
  47.7 6.2 conditional.8
  60.8 6.2 conditional.8
  73.6 4.7 collective-permute-start
  78.3 3.3 collective-permute-start.1
  81.7 2.1 collective-permute-done.1
  83.9 154.5 %while.85 = (s32[]{:T(128)}, bf16[64,768]{1,0:T(8,128)(2,1)S(1)}, bf16[3,64,768]{2,1,0:T(8,128)(2,1)S(1)}, bf16[3,64,768]{2,1,0:T(8,128)(2,1)S(1)}, s32[]{:T(128...) while((s32[]{:T(128)}, bf16[64,768]{1,0:T(8,128)(2,1)S(1)}, ...), condition=%wide.region_9.10_spmd, body=%wide.region_5.9_spmd.sunk | while | flops 89710664 | bytes 4455965 | solution.py:105
  86.5 6.4 %collective-permute-start.3 = (bf16[64,768]{1,0:T(8,128)(2,1)S(1)}, bf16[64,768]{1,0:T(8,128)(2,1)S(1)}, u32[]{:S(2)}, u32[]{:S(2)}) collective-permute-start(bf16[64,768]{1,0:T(8,128)(2,1)S(1)} %get-tuple-element.1691), channel_id=1, source_target_pairs={{0,12},{1,13},{2,14},{3,15},{16,28},{17,29},{18,30},{19,31},{32,44... | collective-permute-start | bytes 294920 | tf_op jit(solution)/shard_map/while/body/eval_jaxpr/ppermute | solution.py:11
  93.0 2.1 collective-permute-done.3
  97.8 6.5 %collective-permute-start.3 = (bf16[64,768]{1,0:T(8,128)(2,1)S(1)}, bf16[64,768]{1,0:T(8,128)(2,1)S(1)}, u32[]{:S(2)}, u32[]{:S(2)}) collective-permute-start(bf16[64,768]{1,0:T(8,128)(2,1)S(1)} %get-tuple-element.1691), channel_id=1, source_target_pairs={{0,12},{1,13},{2,14},{3,15},{16,28},{17,29},{18,30},{19,31},{32,44... | collective-permute-start | bytes 294920 | tf_op jit(solution)/shard_map/while/body/eval_jaxpr/ppermute | solution.py:11
  104.4 2.1 collective-permute-done.3
  109.2 6.5 %collective-permute-start.3 = (bf16[64,768]{1,0:T(8,128)(2,1)S(1)}, bf16[64,768]{1,0:T(8,128)(2,1)S(1)}, u32[]{:S(2)}, u32[]{:S(2)}) collective-permute-start(bf16[64,768]{1,0:T(8,128)(2,1)S(1)} %get-tuple-element.1691), channel_id=1, source_target_pairs={{0,12},{1,13},{2,14},{3,15},{16,28},{17,29},{18,30},{19,31},{32,44... | collective-permute-start | bytes 294920 | tf_op jit(solution)/shard_map/while/body/eval_jaxpr/ppermute | solution.py:11
  115.8 2.1 collective-permute-done.3
  120.6 6.5 %collective-permute-start.3 = (bf16[64,768]{1,0:T(8,128)(2,1)S(1)}, bf16[64,768]{1,0:T(8,128)(2,1)S(1)}, u32[]{:S(2)}, u32[]{:S(2)}) collective-permute-start(bf16[64,768]{1,0:T(8,128)(2,1)S(1)} %get-tuple-element.1691), channel_id=1, source_target_pairs={{0,12},{1,13},{2,14},{3,15},{16,28},{17,29},{18,30},{19,31},{32,44... | collective-permute-start | bytes 294920 | tf_op jit(solution)/shard_map/while/body/eval_jaxpr/ppermute | solution.py:11
  127.2 2.1 collective-permute-done.3
  132.0 6.5 %collective-permute-start.3 = (bf16[64,768]{1,0:T(8,128)(2,1)S(1)}, bf16[64,768]{1,0:T(8,128)(2,1)S(1)}, u32[]{:S(2)}, u32[]{:S(2)}) collective-permute-start(bf16[64,768]{1,0:T(8,128)(2,1)S(1)} %get-tuple-element.1691), channel_id=1, source_target_pairs={{0,12},{1,13},{2,14},{3,15},{16,28},{17,29},{18,30},{19,31},{32,44... | collective-permute-start | bytes 294920 | tf_op jit(solution)/shard_map/while/body/eval_jaxpr/ppermute | solution.py:11
  138.6 2.1 collective-permute-done.3
  143.4 6.5 %collective-permute-start.3 = (bf16[64,768]{1,0:T(8,128)(2,1)S(1)}, bf16[64,768]{1,0:T(8,128)(2,1)S(1)}, u32[]{:S(2)}, u32[]{:S(2)}) collective-permute-start(bf16[64,768]{1,0:T(8,128)(2,1)S(1)} %get-tuple-element.1691), channel_id=1, source_target_pairs={{0,12},{1,13},{2,14},{3,15},{16,28},{17,29},{18,30},{19,31},{32,44... | collective-permute-start | bytes 294920 | tf_op jit(solution)/shard_map/while/body/eval_jaxpr/ppermute | solution.py:11
  150.0 2.1 collective-permute-done.3
  154.8 6.5 %collective-permute-start.3 = (bf16[64,768]{1,0:T(8,128)(2,1)S(1)}, bf16[64,768]{1,0:T(8,128)(2,1)S(1)}, u32[]{:S(2)}, u32[]{:S(2)}) collective-permute-start(bf16[64,768]{1,0:T(8,128)(2,1)S(1)} %get-tuple-element.1691), channel_id=1, source_target_pairs={{0,12},{1,13},{2,14},{3,15},{16,28},{17,29},{18,30},{19,31},{32,44... | collective-permute-start | bytes 294920 | tf_op jit(solution)/shard_map/while/body/eval_jaxpr/ppermute | solution.py:11
  161.4 2.1 collective-permute-done.3
  166.2 6.5 %collective-permute-start.3 = (bf16[64,768]{1,0:T(8,128)(2,1)S(1)}, bf16[64,768]{1,0:T(8,128)(2,1)S(1)}, u32[]{:S(2)}, u32[]{:S(2)}) collective-permute-start(bf16[64,768]{1,0:T(8,128)(2,1)S(1)} %get-tuple-element.1691), channel_id=1, source_target_pairs={{0,12},{1,13},{2,14},{3,15},{16,28},{17,29},{18,30},{19,31},{32,44... | collective-permute-start | bytes 294920 | tf_op jit(solution)/shard_map/while/body/eval_jaxpr/ppermute | solution.py:11
  172.8 2.1 collective-permute-done.3
  177.6 13.4 %collective-permute-start.3 = (bf16[64,768]{1,0:T(8,128)(2,1)S(1)}, bf16[64,768]{1,0:T(8,128)(2,1)S(1)}, u32[]{:S(2)}, u32[]{:S(2)}) collective-permute-start(bf16[64,768]{1,0:T(8,128)(2,1)S(1)} %get-tuple-element.1691), channel_id=1, source_target_pairs={{0,12},{1,13},{2,14},{3,15},{16,28},{17,29},{18,30},{19,31},{32,44... | collective-permute-start | bytes 294920 | tf_op jit(solution)/shard_map/while/body/eval_jaxpr/ppermute | solution.py:11
  191.1 2.1 collective-permute-done.3
  195.9 12.0 %collective-permute-start.3 = (bf16[64,768]{1,0:T(8,128)(2,1)S(1)}, bf16[64,768]{1,0:T(8,128)(2,1)S(1)}, u32[]{:S(2)}, u32[]{:S(2)}) collective-permute-start(bf16[64,768]{1,0:T(8,128)(2,1)S(1)} %get-tuple-element.1691), channel_id=1, source_target_pairs={{0,12},{1,13},{2,14},{3,15},{16,28},{17,29},{18,30},{19,31},{32,44... | collective-permute-start | bytes 294920 | tf_op jit(solution)/shard_map/while/body/eval_jaxpr/ppermute | solution.py:11
  208.0 2.1 collective-permute-done.3
  212.8 12.0 %collective-permute-start.3 = (bf16[64,768]{1,0:T(8,128)(2,1)S(1)}, bf16[64,768]{1,0:T(8,128)(2,1)S(1)}, u32[]{:S(2)}, u32[]{:S(2)}) collective-permute-start(bf16[64,768]{1,0:T(8,128)(2,1)S(1)} %get-tuple-element.1691), channel_id=1, source_target_pairs={{0,12},{1,13},{2,14},{3,15},{16,28},{17,29},{18,30},{19,31},{32,44... | collective-permute-start | bytes 294920 | tf_op jit(solution)/shard_map/while/body/eval_jaxpr/ppermute | solution.py:11
  224.8 2.1 collective-permute-done.3
  229.6 6.5 %collective-permute-start.3 = (bf16[64,768]{1,0:T(8,128)(2,1)S(1)}, bf16[64,768]{1,0:T(8,128)(2,1)S(1)}, u32[]{:S(2)}, u32[]{:S(2)}) collective-permute-start(bf16[64,768]{1,0:T(8,128)(2,1)S(1)} %get-tuple-element.1691), channel_id=1, source_target_pairs={{0,12},{1,13},{2,14},{3,15},{16,28},{17,29},{18,30},{19,31},{32,44... | collective-permute-start | bytes 294920 | tf_op jit(solution)/shard_map/while/body/eval_jaxpr/ppermute | solution.py:11
  236.2 2.1 collective-permute-done.3
  239.1 73.2 %while.86 = (s32[]{:T(128)}, bf16[64,768]{1,0:T(8,128)(2,1)S(1)}, bf16[3,64,768]{2,1,0:T(8,128)(2,1)S(1)}, f32[768,768]{1,0:T(8,128)S(1)}, s32[]{:T(128)}, /*ind...) while((s32[]{:T(128)}, bf16[64,768]{1,0:T(8,128)(2,1)S(1)}, ...), condition=%wide.region_15.16_spmd, body=%wide.region_10.15_spmd.sunk | while | flops 155271552 | bytes 11747327 | solution.py:148
  239.1 3.8 collective-permute-start.4
  244.2 7.3 %collective-permute-done.5 = bf16[64,768]{1,0:T(8,128)(2,1)S(1)} collective-permute-done((bf16[64,768]{1,0:T(8,128)(2,1)S(1)}, bf16[64,768]{1,0:T(8,128)(2,1)S(1)}, u32[]{:S(2)}, u32[]{:S(2)}) %collective-permute-start.5) | collective-permute-done | bytes 98336 | tf_op jit(solution)/shard_map/while/body/eval_jaxpr/ppermute | solution.py:11
  251.6 4.3 collective-permute-start.4
  257.3 8.7 %collective-permute-done.5 = bf16[64,768]{1,0:T(8,128)(2,1)S(1)} collective-permute-done((bf16[64,768]{1,0:T(8,128)(2,1)S(1)}, bf16[64,768]{1,0:T(8,128)(2,1)S(1)}, u32[]{:S(2)}, u32[]{:S(2)}) %collective-permute-start.5) | collective-permute-done | bytes 98336 | tf_op jit(solution)/shard_map/while/body/eval_jaxpr/ppermute | solution.py:11
  269.3 8.7 %collective-permute-done.5 = bf16[64,768]{1,0:T(8,128)(2,1)S(1)} collective-permute-done((bf16[64,768]{1,0:T(8,128)(2,1)S(1)}, bf16[64,768]{1,0:T(8,128)(2,1)S(1)}, u32[]{:S(2)}, u32[]{:S(2)}) %collective-permute-start.5) | collective-permute-done | bytes 98336 | tf_op jit(solution)/shard_map/while/body/eval_jaxpr/ppermute | solution.py:11
  281.4 8.1 %collective-permute-done.5 = bf16[64,768]{1,0:T(8,128)(2,1)S(1)} collective-permute-done((bf16[64,768]{1,0:T(8,128)(2,1)S(1)}, bf16[64,768]{1,0:T(8,128)(2,1)S(1)}, u32[]{:S(2)}, u32[]{:S(2)}) %collective-permute-start.5) | collective-permute-done | bytes 98336 | tf_op jit(solution)/shard_map/while/body/eval_jaxpr/ppermute | solution.py:11
  292.9 8.1 %collective-permute-done.5 = bf16[64,768]{1,0:T(8,128)(2,1)S(1)} collective-permute-done((bf16[64,768]{1,0:T(8,128)(2,1)S(1)}, bf16[64,768]{1,0:T(8,128)(2,1)S(1)}, u32[]{:S(2)}, u32[]{:S(2)}) %collective-permute-start.5) | collective-permute-done | bytes 98336 | tf_op jit(solution)/shard_map/while/body/eval_jaxpr/ppermute | solution.py:11
  304.4 7.9 %collective-permute-done.5 = bf16[64,768]{1,0:T(8,128)(2,1)S(1)} collective-permute-done((bf16[64,768]{1,0:T(8,128)(2,1)S(1)}, bf16[64,768]{1,0:T(8,128)(2,1)S(1)}, u32[]{:S(2)}, u32[]{:S(2)}) %collective-permute-start.5) | collective-permute-done | bytes 98336 | tf_op jit(solution)/shard_map/while/body/eval_jaxpr/ppermute | solution.py:11
  312.3 148.8 %while.87 = (s32[]{:T(128)}, bf16[64,768]{1,0:T(8,128)(2,1)S(1)}, bf16[3,64,768]{2,1,0:T(8,128)(2,1)S(1)}, f32[768,768]{1,0:T(8,128)S(1)}, s32[]{:T(128)}, /*ind...) while((s32[]{:T(128)}, bf16[64,768]{1,0:T(8,128)(2,1)S(1)}, ...), condition=%wide.region_21.22_spmd, body=%wide.region_16.21_spmd.sunk | while | flops 155271552 | bytes 11747347 | solution.py:149
  315.6 7.9 %collective-permute-done.7 = bf16[64,768]{1,0:T(8,128)(2,1)S(1)} collective-permute-done((bf16[64,768]{1,0:T(8,128)(2,1)S(1)}, bf16[64,768]{1,0:T(8,128)(2,1)S(1)}, u32[]{:S(2)}, u32[]{:S(2)}) %collective-permute-start.7) | collective-permute-done | bytes 98336 | tf_op jit(solution)/shard_map/while/body/eval_jaxpr/ppermute | solution.py:11
  326.9 7.9 %collective-permute-done.7 = bf16[64,768]{1,0:T(8,128)(2,1)S(1)} collective-permute-done((bf16[64,768]{1,0:T(8,128)(2,1)S(1)}, bf16[64,768]{1,0:T(8,128)(2,1)S(1)}, u32[]{:S(2)}, u32[]{:S(2)}) %collective-permute-start.7) | collective-permute-done | bytes 98336 | tf_op jit(solution)/shard_map/while/body/eval_jaxpr/ppermute | solution.py:11
  338.1 7.9 %collective-permute-done.7 = bf16[64,768]{1,0:T(8,128)(2,1)S(1)} collective-permute-done((bf16[64,768]{1,0:T(8,128)(2,1)S(1)}, bf16[64,768]{1,0:T(8,128)(2,1)S(1)}, u32[]{:S(2)}, u32[]{:S(2)}) %collective-permute-start.7) | collective-permute-done | bytes 98336 | tf_op jit(solution)/shard_map/while/body/eval_jaxpr/ppermute | solution.py:11
  349.3 7.9 %collective-permute-done.7 = bf16[64,768]{1,0:T(8,128)(2,1)S(1)} collective-permute-done((bf16[64,768]{1,0:T(8,128)(2,1)S(1)}, bf16[64,768]{1,0:T(8,128)(2,1)S(1)}, u32[]{:S(2)}, u32[]{:S(2)}) %collective-permute-start.7) | collective-permute-done | bytes 98336 | tf_op jit(solution)/shard_map/while/body/eval_jaxpr/ppermute | solution.py:11
  360.6 7.9 %collective-permute-done.7 = bf16[64,768]{1,0:T(8,128)(2,1)S(1)} collective-permute-done((bf16[64,768]{1,0:T(8,128)(2,1)S(1)}, bf16[64,768]{1,0:T(8,128)(2,1)S(1)}, u32[]{:S(2)}, u32[]{:S(2)}) %collective-permute-start.7) | collective-permute-done | bytes 98336 | tf_op jit(solution)/shard_map/while/body/eval_jaxpr/ppermute | solution.py:11
  371.8 7.9 %collective-permute-done.7 = bf16[64,768]{1,0:T(8,128)(2,1)S(1)} collective-permute-done((bf16[64,768]{1,0:T(8,128)(2,1)S(1)}, bf16[64,768]{1,0:T(8,128)(2,1)S(1)}, u32[]{:S(2)}, u32[]{:S(2)}) %collective-permute-start.7) | collective-permute-done | bytes 98336 | tf_op jit(solution)/shard_map/while/body/eval_jaxpr/ppermute | solution.py:11
  383.1 7.3 %collective-permute-done.7 = bf16[64,768]{1,0:T(8,128)(2,1)S(1)} collective-permute-done((bf16[64,768]{1,0:T(8,128)(2,1)S(1)}, bf16[64,768]{1,0:T(8,128)(2,1)S(1)}, u32[]{:S(2)}, u32[]{:S(2)}) %collective-permute-start.7) | collective-permute-done | bytes 98336 | tf_op jit(solution)/shard_map/while/body/eval_jaxpr/ppermute | solution.py:11
  390.4 5.2 conditional.11
  398.9 7.3 %collective-permute-done.7 = bf16[64,768]{1,0:T(8,128)(2,1)S(1)} collective-permute-done((bf16[64,768]{1,0:T(8,128)(2,1)S(1)}, bf16[64,768]{1,0:T(8,128)(2,1)S(1)}, u32[]{:S(2)}, u32[]{:S(2)}) %collective-permute-start.7) | collective-permute-done | bytes 98336 | tf_op jit(solution)/shard_map/while/body/eval_jaxpr/ppermute | solution.py:11
  406.2 5.2 conditional.11
  414.7 7.3 %collective-permute-done.7 = bf16[64,768]{1,0:T(8,128)(2,1)S(1)} collective-permute-done((bf16[64,768]{1,0:T(8,128)(2,1)S(1)}, bf16[64,768]{1,0:T(8,128)(2,1)S(1)}, u32[]{:S(2)}, u32[]{:S(2)}) %collective-permute-start.7) | collective-permute-done | bytes 98336 | tf_op jit(solution)/shard_map/while/body/eval_jaxpr/ppermute | solution.py:11
  422.0 5.2 conditional.11
  430.5 7.9 %collective-permute-done.7 = bf16[64,768]{1,0:T(8,128)(2,1)S(1)} collective-permute-done((bf16[64,768]{1,0:T(8,128)(2,1)S(1)}, bf16[64,768]{1,0:T(8,128)(2,1)S(1)}, u32[]{:S(2)}, u32[]{:S(2)}) %collective-permute-start.7) | collective-permute-done | bytes 98336 | tf_op jit(solution)/shard_map/while/body/eval_jaxpr/ppermute | solution.py:11
  441.7 8.1 %collective-permute-done.7 = bf16[64,768]{1,0:T(8,128)(2,1)S(1)} collective-permute-done((bf16[64,768]{1,0:T(8,128)(2,1)S(1)}, bf16[64,768]{1,0:T(8,128)(2,1)S(1)}, u32[]{:S(2)}, u32[]{:S(2)}) %collective-permute-start.7) | collective-permute-done | bytes 98336 | tf_op jit(solution)/shard_map/while/body/eval_jaxpr/ppermute | solution.py:11
  453.2 7.9 %collective-permute-done.7 = bf16[64,768]{1,0:T(8,128)(2,1)S(1)} collective-permute-done((bf16[64,768]{1,0:T(8,128)(2,1)S(1)}, bf16[64,768]{1,0:T(8,128)(2,1)S(1)}, u32[]{:S(2)}, u32[]{:S(2)}) %collective-permute-start.7) | collective-permute-done | bytes 98336 | tf_op jit(solution)/shard_map/while/body/eval_jaxpr/ppermute | solution.py:11
  462.6 162.6 %all-reduce.12.cloned.1.call-done = f32[768,768]{1,0:T(8,128)} async-done(((f32[768,768]{1,0:T(8,128)}), f32[768,768]{1,0:T(8,128)}) %all-reduce.12.cloned.1.call-update) | async-done | bytes 2359312 | tf_op jit(solution)/shard_map/psum | solution.py:150
  625.1 3.3 multiply_bitcast_fusion
  (333 shorter events, 158.9 us)
Async XLA Ops:
  6.5 618.6 %all-reduce.12.cloned.1.call-start = ((), (), s32[]{:S(2)}) async-start(), calls=%async_computation | async-start | bytes 4718592 | tf_op jit(solution)/shard_map/psum | solution.py:150
  8.0 14.2 %collective-permute-start = (bf16[64,768]{1,0:T(8,128)(2,1)S(1)}, bf16[64,768]{1,0:T(8,128)(2,1)S(1)}, u32[]{:S(2)}, u32[]{:S(2)}) collective-permute-start(bf16[64,768]{1,0:T(8,128)(2,1)S(1)} %get-tuple-element.1675), channel_id=1, source_target_pairs={{0,1},{1,2},{2,3},{3,4},{4,5},{5,6},{6,7},{7,8},{8,9},{9,10},{10,1... | collective-permute-start | bytes 294920 | tf_op jit(solution)/shard_map/while/body/eval_jaxpr/ppermute | solution.py:11
  9.9 12.2 %collective-permute-start.1 = (bf16[64,768]{1,0:T(8,128)(2,1)S(1)}, bf16[64,768]{1,0:T(8,128)(2,1)S(1)}, u32[]{:S(2)}, u32[]{:S(2)}) collective-permute-start(bf16[64,768]{1,0:T(8,128)(2,1)S(1)} %get-tuple-element.1675), channel_id=1, source_target_pairs={{0,12},{1,13},{2,14},{3,15},{16,28},{17,29},{18,30},{19,31},{32,44... | collective-permute-start | bytes 294920 | tf_op jit(solution)/shard_map/while/body/eval_jaxpr/ppermute | solution.py:11
  22.9 12.6 %collective-permute-start = (bf16[64,768]{1,0:T(8,128)(2,1)S(1)}, bf16[64,768]{1,0:T(8,128)(2,1)S(1)}, u32[]{:S(2)}, u32[]{:S(2)}) collective-permute-start(bf16[64,768]{1,0:T(8,128)(2,1)S(1)} %get-tuple-element.1675), channel_id=1, source_target_pairs={{0,1},{1,2},{2,3},{3,4},{4,5},{5,6},{6,7},{7,8},{8,9},{9,10},{10,1... | collective-permute-start | bytes 294920 | tf_op jit(solution)/shard_map/while/body/eval_jaxpr/ppermute | solution.py:11
  24.9 8.7 %collective-permute-start.1 = (bf16[64,768]{1,0:T(8,128)(2,1)S(1)}, bf16[64,768]{1,0:T(8,128)(2,1)S(1)}, u32[]{:S(2)}, u32[]{:S(2)}) collective-permute-start(bf16[64,768]{1,0:T(8,128)(2,1)S(1)} %get-tuple-element.1675), channel_id=1, source_target_pairs={{0,12},{1,13},{2,14},{3,15},{16,28},{17,29},{18,30},{19,31},{32,44... | collective-permute-start | bytes 294920 | tf_op jit(solution)/shard_map/while/body/eval_jaxpr/ppermute | solution.py:11
  73.6 10.2 %collective-permute-start = (bf16[64,768]{1,0:T(8,128)(2,1)S(1)}, bf16[64,768]{1,0:T(8,128)(2,1)S(1)}, u32[]{:S(2)}, u32[]{:S(2)}) collective-permute-start(bf16[64,768]{1,0:T(8,128)(2,1)S(1)} %get-tuple-element.1675), channel_id=1, source_target_pairs={{0,1},{1,2},{2,3},{3,4},{4,5},{5,6},{6,7},{7,8},{8,9},{9,10},{10,1... | collective-permute-start | bytes 294920 | tf_op jit(solution)/shard_map/while/body/eval_jaxpr/ppermute | solution.py:11
  84.6 10.6 %collective-permute-start.2 = (bf16[64,768]{1,0:T(8,128)(2,1)S(1)}, bf16[64,768]{1,0:T(8,128)(2,1)S(1)}, u32[]{:S(2)}, u32[]{:S(2)}) collective-permute-start(bf16[64,768]{1,0:T(8,128)(2,1)S(1)} %get-tuple-element.1691), channel_id=1, source_target_pairs={{0,1},{1,2},{2,3},{3,4},{4,5},{5,6},{6,7},{7,8},{8,9},{9,10},{10,1... | collective-permute-start | bytes 294920 | tf_op jit(solution)/shard_map/while/body/eval_jaxpr/ppermute | solution.py:11
  86.5 8.6 %collective-permute-start.3 = (bf16[64,768]{1,0:T(8,128)(2,1)S(1)}, bf16[64,768]{1,0:T(8,128)(2,1)S(1)}, u32[]{:S(2)}, u32[]{:S(2)}) collective-permute-start(bf16[64,768]{1,0:T(8,128)(2,1)S(1)} %get-tuple-element.1691), channel_id=1, source_target_pairs={{0,12},{1,13},{2,14},{3,15},{16,28},{17,29},{18,30},{19,31},{32,44... | collective-permute-start | bytes 294920 | tf_op jit(solution)/shard_map/while/body/eval_jaxpr/ppermute | solution.py:11
  95.9 10.7 %collective-permute-start.2 = (bf16[64,768]{1,0:T(8,128)(2,1)S(1)}, bf16[64,768]{1,0:T(8,128)(2,1)S(1)}, u32[]{:S(2)}, u32[]{:S(2)}) collective-permute-start(bf16[64,768]{1,0:T(8,128)(2,1)S(1)} %get-tuple-element.1691), channel_id=1, source_target_pairs={{0,1},{1,2},{2,3},{3,4},{4,5},{5,6},{6,7},{7,8},{8,9},{9,10},{10,1... | collective-permute-start | bytes 294920 | tf_op jit(solution)/shard_map/while/body/eval_jaxpr/ppermute | solution.py:11
  97.8 8.7 %collective-permute-start.3 = (bf16[64,768]{1,0:T(8,128)(2,1)S(1)}, bf16[64,768]{1,0:T(8,128)(2,1)S(1)}, u32[]{:S(2)}, u32[]{:S(2)}) collective-permute-start(bf16[64,768]{1,0:T(8,128)(2,1)S(1)} %get-tuple-element.1691), channel_id=1, source_target_pairs={{0,12},{1,13},{2,14},{3,15},{16,28},{17,29},{18,30},{19,31},{32,44... | collective-permute-start | bytes 294920 | tf_op jit(solution)/shard_map/while/body/eval_jaxpr/ppermute | solution.py:11
  107.2 10.7 %collective-permute-start.2 = (bf16[64,768]{1,0:T(8,128)(2,1)S(1)}, bf16[64,768]{1,0:T(8,128)(2,1)S(1)}, u32[]{:S(2)}, u32[]{:S(2)}) collective-permute-start(bf16[64,768]{1,0:T(8,128)(2,1)S(1)} %get-tuple-element.1691), channel_id=1, source_target_pairs={{0,1},{1,2},{2,3},{3,4},{4,5},{5,6},{6,7},{7,8},{8,9},{9,10},{10,1... | collective-permute-start | bytes 294920 | tf_op jit(solution)/shard_map/while/body/eval_jaxpr/ppermute | solution.py:11
  109.2 8.7 %collective-permute-start.3 = (bf16[64,768]{1,0:T(8,128)(2,1)S(1)}, bf16[64,768]{1,0:T(8,128)(2,1)S(1)}, u32[]{:S(2)}, u32[]{:S(2)}) collective-permute-start(bf16[64,768]{1,0:T(8,128)(2,1)S(1)} %get-tuple-element.1691), channel_id=1, source_target_pairs={{0,12},{1,13},{2,14},{3,15},{16,28},{17,29},{18,30},{19,31},{32,44... | collective-permute-start | bytes 294920 | tf_op jit(solution)/shard_map/while/body/eval_jaxpr/ppermute | solution.py:11
  118.6 10.7 %collective-permute-start.2 = (bf16[64,768]{1,0:T(8,128)(2,1)S(1)}, bf16[64,768]{1,0:T(8,128)(2,1)S(1)}, u32[]{:S(2)}, u32[]{:S(2)}) collective-permute-start(bf16[64,768]{1,0:T(8,128)(2,1)S(1)} %get-tuple-element.1691), channel_id=1, source_target_pairs={{0,1},{1,2},{2,3},{3,4},{4,5},{5,6},{6,7},{7,8},{8,9},{9,10},{10,1... | collective-permute-start | bytes 294920 | tf_op jit(solution)/shard_map/while/body/eval_jaxpr/ppermute | solution.py:11
  120.6 8.7 %collective-permute-start.3 = (bf16[64,768]{1,0:T(8,128)(2,1)S(1)}, bf16[64,768]{1,0:T(8,128)(2,1)S(1)}, u32[]{:S(2)}, u32[]{:S(2)}) collective-permute-start(bf16[64,768]{1,0:T(8,128)(2,1)S(1)} %get-tuple-element.1691), channel_id=1, source_target_pairs={{0,12},{1,13},{2,14},{3,15},{16,28},{17,29},{18,30},{19,31},{32,44... | collective-permute-start | bytes 294920 | tf_op jit(solution)/shard_map/while/body/eval_jaxpr/ppermute | solution.py:11
  130.0 10.7 %collective-permute-start.2 = (bf16[64,768]{1,0:T(8,128)(2,1)S(1)}, bf16[64,768]{1,0:T(8,128)(2,1)S(1)}, u32[]{:S(2)}, u32[]{:S(2)}) collective-permute-start(bf16[64,768]{1,0:T(8,128)(2,1)S(1)} %get-tuple-element.1691), channel_id=1, source_target_pairs={{0,1},{1,2},{2,3},{3,4},{4,5},{5,6},{6,7},{7,8},{8,9},{9,10},{10,1... | collective-permute-start | bytes 294920 | tf_op jit(solution)/shard_map/while/body/eval_jaxpr/ppermute | solution.py:11
  132.0 8.7 %collective-permute-start.3 = (bf16[64,768]{1,0:T(8,128)(2,1)S(1)}, bf16[64,768]{1,0:T(8,128)(2,1)S(1)}, u32[]{:S(2)}, u32[]{:S(2)}) collective-permute-start(bf16[64,768]{1,0:T(8,128)(2,1)S(1)} %get-tuple-element.1691), channel_id=1, source_target_pairs={{0,12},{1,13},{2,14},{3,15},{16,28},{17,29},{18,30},{19,31},{32,44... | collective-permute-start | bytes 294920 | tf_op jit(solution)/shard_map/while/body/eval_jaxpr/ppermute | solution.py:11
  141.4 10.7 %collective-permute-start.2 = (bf16[64,768]{1,0:T(8,128)(2,1)S(1)}, bf16[64,768]{1,0:T(8,128)(2,1)S(1)}, u32[]{:S(2)}, u32[]{:S(2)}) collective-permute-start(bf16[64,768]{1,0:T(8,128)(2,1)S(1)} %get-tuple-element.1691), channel_id=1, source_target_pairs={{0,1},{1,2},{2,3},{3,4},{4,5},{5,6},{6,7},{7,8},{8,9},{9,10},{10,1... | collective-permute-start | bytes 294920 | tf_op jit(solution)/shard_map/while/body/eval_jaxpr/ppermute | solution.py:11
  143.4 8.7 %collective-permute-start.3 = (bf16[64,768]{1,0:T(8,128)(2,1)S(1)}, bf16[64,768]{1,0:T(8,128)(2,1)S(1)}, u32[]{:S(2)}, u32[]{:S(2)}) collective-permute-start(bf16[64,768]{1,0:T(8,128)(2,1)S(1)} %get-tuple-element.1691), channel_id=1, source_target_pairs={{0,12},{1,13},{2,14},{3,15},{16,28},{17,29},{18,30},{19,31},{32,44... | collective-permute-start | bytes 294920 | tf_op jit(solution)/shard_map/while/body/eval_jaxpr/ppermute | solution.py:11
  152.8 10.7 %collective-permute-start.2 = (bf16[64,768]{1,0:T(8,128)(2,1)S(1)}, bf16[64,768]{1,0:T(8,128)(2,1)S(1)}, u32[]{:S(2)}, u32[]{:S(2)}) collective-permute-start(bf16[64,768]{1,0:T(8,128)(2,1)S(1)} %get-tuple-element.1691), channel_id=1, source_target_pairs={{0,1},{1,2},{2,3},{3,4},{4,5},{5,6},{6,7},{7,8},{8,9},{9,10},{10,1... | collective-permute-start | bytes 294920 | tf_op jit(solution)/shard_map/while/body/eval_jaxpr/ppermute | solution.py:11
  154.8 8.7 %collective-permute-start.3 = (bf16[64,768]{1,0:T(8,128)(2,1)S(1)}, bf16[64,768]{1,0:T(8,128)(2,1)S(1)}, u32[]{:S(2)}, u32[]{:S(2)}) collective-permute-start(bf16[64,768]{1,0:T(8,128)(2,1)S(1)} %get-tuple-element.1691), channel_id=1, source_target_pairs={{0,12},{1,13},{2,14},{3,15},{16,28},{17,29},{18,30},{19,31},{32,44... | collective-permute-start | bytes 294920 | tf_op jit(solution)/shard_map/while/body/eval_jaxpr/ppermute | solution.py:11
  164.2 10.7 %collective-permute-start.2 = (bf16[64,768]{1,0:T(8,128)(2,1)S(1)}, bf16[64,768]{1,0:T(8,128)(2,1)S(1)}, u32[]{:S(2)}, u32[]{:S(2)}) collective-permute-start(bf16[64,768]{1,0:T(8,128)(2,1)S(1)} %get-tuple-element.1691), channel_id=1, source_target_pairs={{0,1},{1,2},{2,3},{3,4},{4,5},{5,6},{6,7},{7,8},{8,9},{9,10},{10,1... | collective-permute-start | bytes 294920 | tf_op jit(solution)/shard_map/while/body/eval_jaxpr/ppermute | solution.py:11
  166.2 8.7 %collective-permute-start.3 = (bf16[64,768]{1,0:T(8,128)(2,1)S(1)}, bf16[64,768]{1,0:T(8,128)(2,1)S(1)}, u32[]{:S(2)}, u32[]{:S(2)}) collective-permute-start(bf16[64,768]{1,0:T(8,128)(2,1)S(1)} %get-tuple-element.1691), channel_id=1, source_target_pairs={{0,12},{1,13},{2,14},{3,15},{16,28},{17,29},{18,30},{19,31},{32,44... | collective-permute-start | bytes 294920 | tf_op jit(solution)/shard_map/while/body/eval_jaxpr/ppermute | solution.py:11
  175.6 17.6 %collective-permute-start.2 = (bf16[64,768]{1,0:T(8,128)(2,1)S(1)}, bf16[64,768]{1,0:T(8,128)(2,1)S(1)}, u32[]{:S(2)}, u32[]{:S(2)}) collective-permute-start(bf16[64,768]{1,0:T(8,128)(2,1)S(1)} %get-tuple-element.1691), channel_id=1, source_target_pairs={{0,1},{1,2},{2,3},{3,4},{4,5},{5,6},{6,7},{7,8},{8,9},{9,10},{10,1... | collective-permute-start | bytes 294920 | tf_op jit(solution)/shard_map/while/body/eval_jaxpr/ppermute | solution.py:11
  177.6 15.6 %collective-permute-start.3 = (bf16[64,768]{1,0:T(8,128)(2,1)S(1)}, bf16[64,768]{1,0:T(8,128)(2,1)S(1)}, u32[]{:S(2)}, u32[]{:S(2)}) collective-permute-start(bf16[64,768]{1,0:T(8,128)(2,1)S(1)} %get-tuple-element.1691), channel_id=1, source_target_pairs={{0,12},{1,13},{2,14},{3,15},{16,28},{17,29},{18,30},{19,31},{32,44... | collective-permute-start | bytes 294920 | tf_op jit(solution)/shard_map/while/body/eval_jaxpr/ppermute | solution.py:11
  194.0 16.1 %collective-permute-start.2 = (bf16[64,768]{1,0:T(8,128)(2,1)S(1)}, bf16[64,768]{1,0:T(8,128)(2,1)S(1)}, u32[]{:S(2)}, u32[]{:S(2)}) collective-permute-start(bf16[64,768]{1,0:T(8,128)(2,1)S(1)} %get-tuple-element.1691), channel_id=1, source_target_pairs={{0,1},{1,2},{2,3},{3,4},{4,5},{5,6},{6,7},{7,8},{8,9},{9,10},{10,1... | collective-permute-start | bytes 294920 | tf_op jit(solution)/shard_map/while/body/eval_jaxpr/ppermute | solution.py:11
  195.9 14.2 %collective-permute-start.3 = (bf16[64,768]{1,0:T(8,128)(2,1)S(1)}, bf16[64,768]{1,0:T(8,128)(2,1)S(1)}, u32[]{:S(2)}, u32[]{:S(2)}) collective-permute-start(bf16[64,768]{1,0:T(8,128)(2,1)S(1)} %get-tuple-element.1691), channel_id=1, source_target_pairs={{0,12},{1,13},{2,14},{3,15},{16,28},{17,29},{18,30},{19,31},{32,44... | collective-permute-start | bytes 294920 | tf_op jit(solution)/shard_map/while/body/eval_jaxpr/ppermute | solution.py:11
  210.8 16.1 %collective-permute-start.2 = (bf16[64,768]{1,0:T(8,128)(2,1)S(1)}, bf16[64,768]{1,0:T(8,128)(2,1)S(1)}, u32[]{:S(2)}, u32[]{:S(2)}) collective-permute-start(bf16[64,768]{1,0:T(8,128)(2,1)S(1)} %get-tuple-element.1691), channel_id=1, source_target_pairs={{0,1},{1,2},{2,3},{3,4},{4,5},{5,6},{6,7},{7,8},{8,9},{9,10},{10,1... | collective-permute-start | bytes 294920 | tf_op jit(solution)/shard_map/while/body/eval_jaxpr/ppermute | solution.py:11
  212.8 14.2 %collective-permute-start.3 = (bf16[64,768]{1,0:T(8,128)(2,1)S(1)}, bf16[64,768]{1,0:T(8,128)(2,1)S(1)}, u32[]{:S(2)}, u32[]{:S(2)}) collective-permute-start(bf16[64,768]{1,0:T(8,128)(2,1)S(1)} %get-tuple-element.1691), channel_id=1, source_target_pairs={{0,12},{1,13},{2,14},{3,15},{16,28},{17,29},{18,30},{19,31},{32,44... | collective-permute-start | bytes 294920 | tf_op jit(solution)/shard_map/while/body/eval_jaxpr/ppermute | solution.py:11
  227.7 10.7 %collective-permute-start.2 = (bf16[64,768]{1,0:T(8,128)(2,1)S(1)}, bf16[64,768]{1,0:T(8,128)(2,1)S(1)}, u32[]{:S(2)}, u32[]{:S(2)}) collective-permute-start(bf16[64,768]{1,0:T(8,128)(2,1)S(1)} %get-tuple-element.1691), channel_id=1, source_target_pairs={{0,1},{1,2},{2,3},{3,4},{4,5},{5,6},{6,7},{7,8},{8,9},{9,10},{10,1... | collective-permute-start | bytes 294920 | tf_op jit(solution)/shard_map/while/body/eval_jaxpr/ppermute | solution.py:11
  229.6 8.7 %collective-permute-start.3 = (bf16[64,768]{1,0:T(8,128)(2,1)S(1)}, bf16[64,768]{1,0:T(8,128)(2,1)S(1)}, u32[]{:S(2)}, u32[]{:S(2)}) collective-permute-start(bf16[64,768]{1,0:T(8,128)(2,1)S(1)} %get-tuple-element.1691), channel_id=1, source_target_pairs={{0,12},{1,13},{2,14},{3,15},{16,28},{17,29},{18,30},{19,31},{32,44... | collective-permute-start | bytes 294920 | tf_op jit(solution)/shard_map/while/body/eval_jaxpr/ppermute | solution.py:11
  239.1 12.4 %collective-permute-start.4 = (bf16[64,768]{1,0:T(8,128)(2,1)S(1)}, bf16[64,768]{1,0:T(8,128)(2,1)S(1)}, u32[]{:S(2)}, u32[]{:S(2)}) collective-permute-start(bf16[64,768]{1,0:T(8,128)(2,1)S(1)} %get-tuple-element.1709), channel_id=1, source_target_pairs={{1,0},{2,1},{3,2},{4,3},{5,4},{6,5},{7,6},{8,7},{9,8},{10,9},{11,1... | collective-permute-start | bytes 294920 | tf_op jit(solution)/shard_map/while/body/eval_jaxpr/ppermute | solution.py:11
  242.9 8.6 %collective-permute-start.5 = (bf16[64,768]{1,0:T(8,128)(2,1)S(1)}, bf16[64,768]{1,0:T(8,128)(2,1)S(1)}, u32[]{:S(2)}, u32[]{:S(2)}) collective-permute-start(bf16[64,768]{1,0:T(8,128)(2,1)S(1)} %get-tuple-element.1709), channel_id=1, source_target_pairs={{12,0},{13,1},{14,2},{15,3},{28,16},{29,17},{30,18},{31,19},{44,32... | collective-permute-start | bytes 294920 | tf_op jit(solution)/shard_map/while/body/eval_jaxpr/ppermute | solution.py:11
  251.6 14.4 %collective-permute-start.4 = (bf16[64,768]{1,0:T(8,128)(2,1)S(1)}, bf16[64,768]{1,0:T(8,128)(2,1)S(1)}, u32[]{:S(2)}, u32[]{:S(2)}) collective-permute-start(bf16[64,768]{1,0:T(8,128)(2,1)S(1)} %get-tuple-element.1709), channel_id=1, source_target_pairs={{1,0},{2,1},{3,2},{4,3},{5,4},{6,5},{7,6},{8,7},{9,8},{10,9},{11,1... | collective-permute-start | bytes 294920 | tf_op jit(solution)/shard_map/while/body/eval_jaxpr/ppermute | solution.py:11
  255.9 10.0 %collective-permute-start.5 = (bf16[64,768]{1,0:T(8,128)(2,1)S(1)}, bf16[64,768]{1,0:T(8,128)(2,1)S(1)}, u32[]{:S(2)}, u32[]{:S(2)}) collective-permute-start(bf16[64,768]{1,0:T(8,128)(2,1)S(1)} %get-tuple-element.1709), channel_id=1, source_target_pairs={{12,0},{13,1},{14,2},{15,3},{28,16},{29,17},{30,18},{31,19},{44,32... | collective-permute-start | bytes 294920 | tf_op jit(solution)/shard_map/while/body/eval_jaxpr/ppermute | solution.py:11
  266.1 12.0 %collective-permute-start.4 = (bf16[64,768]{1,0:T(8,128)(2,1)S(1)}, bf16[64,768]{1,0:T(8,128)(2,1)S(1)}, u32[]{:S(2)}, u32[]{:S(2)}) collective-permute-start(bf16[64,768]{1,0:T(8,128)(2,1)S(1)} %get-tuple-element.1709), channel_id=1, source_target_pairs={{1,0},{2,1},{3,2},{4,3},{5,4},{6,5},{7,6},{8,7},{9,8},{10,9},{11,1... | collective-permute-start | bytes 294920 | tf_op jit(solution)/shard_map/while/body/eval_jaxpr/ppermute | solution.py:11
  268.0 10.0 %collective-permute-start.5 = (bf16[64,768]{1,0:T(8,128)(2,1)S(1)}, bf16[64,768]{1,0:T(8,128)(2,1)S(1)}, u32[]{:S(2)}, u32[]{:S(2)}) collective-permute-start(bf16[64,768]{1,0:T(8,128)(2,1)S(1)} %get-tuple-element.1709), channel_id=1, source_target_pairs={{12,0},{13,1},{14,2},{15,3},{28,16},{29,17},{30,18},{31,19},{44,32... | collective-permute-start | bytes 294920 | tf_op jit(solution)/shard_map/while/body/eval_jaxpr/ppermute | solution.py:11
  278.1 11.4 %collective-permute-start.4 = (bf16[64,768]{1,0:T(8,128)(2,1)S(1)}, bf16[64,768]{1,0:T(8,128)(2,1)S(1)}, u32[]{:S(2)}, u32[]{:S(2)}) collective-permute-start(bf16[64,768]{1,0:T(8,128)(2,1)S(1)} %get-tuple-element.1709), channel_id=1, source_target_pairs={{1,0},{2,1},{3,2},{4,3},{5,4},{6,5},{7,6},{8,7},{9,8},{10,9},{11,1... | collective-permute-start | bytes 294920 | tf_op jit(solution)/shard_map/while/body/eval_jaxpr/ppermute | solution.py:11
  280.1 9.5 %collective-permute-start.5 = (bf16[64,768]{1,0:T(8,128)(2,1)S(1)}, bf16[64,768]{1,0:T(8,128)(2,1)S(1)}, u32[]{:S(2)}, u32[]{:S(2)}) collective-permute-start(bf16[64,768]{1,0:T(8,128)(2,1)S(1)} %get-tuple-element.1709), channel_id=1, source_target_pairs={{12,0},{13,1},{14,2},{15,3},{28,16},{29,17},{30,18},{31,19},{44,32... | collective-permute-start | bytes 294920 | tf_op jit(solution)/shard_map/while/body/eval_jaxpr/ppermute | solution.py:11
  289.6 11.4 %collective-permute-start.4 = (bf16[64,768]{1,0:T(8,128)(2,1)S(1)}, bf16[64,768]{1,0:T(8,128)(2,1)S(1)}, u32[]{:S(2)}, u32[]{:S(2)}) collective-permute-start(bf16[64,768]{1,0:T(8,128)(2,1)S(1)} %get-tuple-element.1709), channel_id=1, source_target_pairs={{1,0},{2,1},{3,2},{4,3},{5,4},{6,5},{7,6},{8,7},{9,8},{10,9},{11,1... | collective-permute-start | bytes 294920 | tf_op jit(solution)/shard_map/while/body/eval_jaxpr/ppermute | solution.py:11
  291.5 9.4 %collective-permute-start.5 = (bf16[64,768]{1,0:T(8,128)(2,1)S(1)}, bf16[64,768]{1,0:T(8,128)(2,1)S(1)}, u32[]{:S(2)}, u32[]{:S(2)}) collective-permute-start(bf16[64,768]{1,0:T(8,128)(2,1)S(1)} %get-tuple-element.1709), channel_id=1, source_target_pairs={{12,0},{13,1},{14,2},{15,3},{28,16},{29,17},{30,18},{31,19},{44,32... | collective-permute-start | bytes 294920 | tf_op jit(solution)/shard_map/while/body/eval_jaxpr/ppermute | solution.py:11
  301.1 11.2 %collective-permute-start.4 = (bf16[64,768]{1,0:T(8,128)(2,1)S(1)}, bf16[64,768]{1,0:T(8,128)(2,1)S(1)}, u32[]{:S(2)}, u32[]{:S(2)}) collective-permute-start(bf16[64,768]{1,0:T(8,128)(2,1)S(1)} %get-tuple-element.1709), channel_id=1, source_target_pairs={{1,0},{2,1},{3,2},{4,3},{5,4},{6,5},{7,6},{8,7},{9,8},{10,9},{11,1... | collective-permute-start | bytes 294920 | tf_op jit(solution)/shard_map/while/body/eval_jaxpr/ppermute | solution.py:11
  303.0 9.2 %collective-permute-start.5 = (bf16[64,768]{1,0:T(8,128)(2,1)S(1)}, bf16[64,768]{1,0:T(8,128)(2,1)S(1)}, u32[]{:S(2)}, u32[]{:S(2)}) collective-permute-start(bf16[64,768]{1,0:T(8,128)(2,1)S(1)} %get-tuple-element.1709), channel_id=1, source_target_pairs={{12,0},{13,1},{14,2},{15,3},{28,16},{29,17},{30,18},{31,19},{44,32... | collective-permute-start | bytes 294920 | tf_op jit(solution)/shard_map/while/body/eval_jaxpr/ppermute | solution.py:11
  312.3 11.2 %collective-permute-start.6 = (bf16[64,768]{1,0:T(8,128)(2,1)S(1)}, bf16[64,768]{1,0:T(8,128)(2,1)S(1)}, u32[]{:S(2)}, u32[]{:S(2)}) collective-permute-start(bf16[64,768]{1,0:T(8,128)(2,1)S(1)} %get-tuple-element.1725), channel_id=1, source_target_pairs={{1,0},{2,1},{3,2},{4,3},{5,4},{6,5},{7,6},{8,7},{9,8},{10,9},{11,1... | collective-permute-start | bytes 294920 | tf_op jit(solution)/shard_map/while/body/eval_jaxpr/ppermute | solution.py:11
  314.3 9.2 %collective-permute-start.7 = (bf16[64,768]{1,0:T(8,128)(2,1)S(1)}, bf16[64,768]{1,0:T(8,128)(2,1)S(1)}, u32[]{:S(2)}, u32[]{:S(2)}) collective-permute-start(bf16[64,768]{1,0:T(8,128)(2,1)S(1)} %get-tuple-element.1725), channel_id=1, source_target_pairs={{12,0},{13,1},{14,2},{15,3},{28,16},{29,17},{30,18},{31,19},{44,32... | collective-permute-start | bytes 294920 | tf_op jit(solution)/shard_map/while/body/eval_jaxpr/ppermute | solution.py:11
  323.6 11.2 %collective-permute-start.6 = (bf16[64,768]{1,0:T(8,128)(2,1)S(1)}, bf16[64,768]{1,0:T(8,128)(2,1)S(1)}, u32[]{:S(2)}, u32[]{:S(2)}) collective-permute-start(bf16[64,768]{1,0:T(8,128)(2,1)S(1)} %get-tuple-element.1725), channel_id=1, source_target_pairs={{1,0},{2,1},{3,2},{4,3},{5,4},{6,5},{7,6},{8,7},{9,8},{10,9},{11,1... | collective-permute-start | bytes 294920 | tf_op jit(solution)/shard_map/while/body/eval_jaxpr/ppermute | solution.py:11
  325.5 9.2 %collective-permute-start.7 = (bf16[64,768]{1,0:T(8,128)(2,1)S(1)}, bf16[64,768]{1,0:T(8,128)(2,1)S(1)}, u32[]{:S(2)}, u32[]{:S(2)}) collective-permute-start(bf16[64,768]{1,0:T(8,128)(2,1)S(1)} %get-tuple-element.1725), channel_id=1, source_target_pairs={{12,0},{13,1},{14,2},{15,3},{28,16},{29,17},{30,18},{31,19},{44,32... | collective-permute-start | bytes 294920 | tf_op jit(solution)/shard_map/while/body/eval_jaxpr/ppermute | solution.py:11
  334.8 11.2 %collective-permute-start.6 = (bf16[64,768]{1,0:T(8,128)(2,1)S(1)}, bf16[64,768]{1,0:T(8,128)(2,1)S(1)}, u32[]{:S(2)}, u32[]{:S(2)}) collective-permute-start(bf16[64,768]{1,0:T(8,128)(2,1)S(1)} %get-tuple-element.1725), channel_id=1, source_target_pairs={{1,0},{2,1},{3,2},{4,3},{5,4},{6,5},{7,6},{8,7},{9,8},{10,9},{11,1... | collective-permute-start | bytes 294920 | tf_op jit(solution)/shard_map/while/body/eval_jaxpr/ppermute | solution.py:11
  336.8 9.2 %collective-permute-start.7 = (bf16[64,768]{1,0:T(8,128)(2,1)S(1)}, bf16[64,768]{1,0:T(8,128)(2,1)S(1)}, u32[]{:S(2)}, u32[]{:S(2)}) collective-permute-start(bf16[64,768]{1,0:T(8,128)(2,1)S(1)} %get-tuple-element.1725), channel_id=1, source_target_pairs={{12,0},{13,1},{14,2},{15,3},{28,16},{29,17},{30,18},{31,19},{44,32... | collective-permute-start | bytes 294920 | tf_op jit(solution)/shard_map/while/body/eval_jaxpr/ppermute | solution.py:11
  346.1 11.2 %collective-permute-start.6 = (bf16[64,768]{1,0:T(8,128)(2,1)S(1)}, bf16[64,768]{1,0:T(8,128)(2,1)S(1)}, u32[]{:S(2)}, u32[]{:S(2)}) collective-permute-start(bf16[64,768]{1,0:T(8,128)(2,1)S(1)} %get-tuple-element.1725), channel_id=1, source_target_pairs={{1,0},{2,1},{3,2},{4,3},{5,4},{6,5},{7,6},{8,7},{9,8},{10,9},{11,1... | collective-permute-start | bytes 294920 | tf_op jit(solution)/shard_map/while/body/eval_jaxpr/ppermute | solution.py:11
  348.0 9.2 %collective-permute-start.7 = (bf16[64,768]{1,0:T(8,128)(2,1)S(1)}, bf16[64,768]{1,0:T(8,128)(2,1)S(1)}, u32[]{:S(2)}, u32[]{:S(2)}) collective-permute-start(bf16[64,768]{1,0:T(8,128)(2,1)S(1)} %get-tuple-element.1725), channel_id=1, source_target_pairs={{12,0},{13,1},{14,2},{15,3},{28,16},{29,17},{30,18},{31,19},{44,32... | collective-permute-start | bytes 294920 | tf_op jit(solution)/shard_map/while/body/eval_jaxpr/ppermute | solution.py:11
  357.3 11.2 %collective-permute-start.6 = (bf16[64,768]{1,0:T(8,128)(2,1)S(1)}, bf16[64,768]{1,0:T(8,128)(2,1)S(1)}, u32[]{:S(2)}, u32[]{:S(2)}) collective-permute-start(bf16[64,768]{1,0:T(8,128)(2,1)S(1)} %get-tuple-element.1725), channel_id=1, source_target_pairs={{1,0},{2,1},{3,2},{4,3},{5,4},{6,5},{7,6},{8,7},{9,8},{10,9},{11,1... | collective-permute-start | bytes 294920 | tf_op jit(solution)/shard_map/while/body/eval_jaxpr/ppermute | solution.py:11
  359.2 9.2 %collective-permute-start.7 = (bf16[64,768]{1,0:T(8,128)(2,1)S(1)}, bf16[64,768]{1,0:T(8,128)(2,1)S(1)}, u32[]{:S(2)}, u32[]{:S(2)}) collective-permute-start(bf16[64,768]{1,0:T(8,128)(2,1)S(1)} %get-tuple-element.1725), channel_id=1, source_target_pairs={{12,0},{13,1},{14,2},{15,3},{28,16},{29,17},{30,18},{31,19},{44,32... | collective-permute-start | bytes 294920 | tf_op jit(solution)/shard_map/while/body/eval_jaxpr/ppermute | solution.py:11
  368.5 11.2 %collective-permute-start.6 = (bf16[64,768]{1,0:T(8,128)(2,1)S(1)}, bf16[64,768]{1,0:T(8,128)(2,1)S(1)}, u32[]{:S(2)}, u32[]{:S(2)}) collective-permute-start(bf16[64,768]{1,0:T(8,128)(2,1)S(1)} %get-tuple-element.1725), channel_id=1, source_target_pairs={{1,0},{2,1},{3,2},{4,3},{5,4},{6,5},{7,6},{8,7},{9,8},{10,9},{11,1... | collective-permute-start | bytes 294920 | tf_op jit(solution)/shard_map/while/body/eval_jaxpr/ppermute | solution.py:11
  370.5 9.2 %collective-permute-start.7 = (bf16[64,768]{1,0:T(8,128)(2,1)S(1)}, bf16[64,768]{1,0:T(8,128)(2,1)S(1)}, u32[]{:S(2)}, u32[]{:S(2)}) collective-permute-start(bf16[64,768]{1,0:T(8,128)(2,1)S(1)} %get-tuple-element.1725), channel_id=1, source_target_pairs={{12,0},{13,1},{14,2},{15,3},{28,16},{29,17},{30,18},{31,19},{44,32... | collective-permute-start | bytes 294920 | tf_op jit(solution)/shard_map/while/body/eval_jaxpr/ppermute | solution.py:11
  379.8 10.6 %collective-permute-start.6 = (bf16[64,768]{1,0:T(8,128)(2,1)S(1)}, bf16[64,768]{1,0:T(8,128)(2,1)S(1)}, u32[]{:S(2)}, u32[]{:S(2)}) collective-permute-start(bf16[64,768]{1,0:T(8,128)(2,1)S(1)} %get-tuple-element.1725), channel_id=1, source_target_pairs={{1,0},{2,1},{3,2},{4,3},{5,4},{6,5},{7,6},{8,7},{9,8},{10,9},{11,1... | collective-permute-start | bytes 294920 | tf_op jit(solution)/shard_map/while/body/eval_jaxpr/ppermute | solution.py:11
  381.7 8.6 %collective-permute-start.7 = (bf16[64,768]{1,0:T(8,128)(2,1)S(1)}, bf16[64,768]{1,0:T(8,128)(2,1)S(1)}, u32[]{:S(2)}, u32[]{:S(2)}) collective-permute-start(bf16[64,768]{1,0:T(8,128)(2,1)S(1)} %get-tuple-element.1725), channel_id=1, source_target_pairs={{12,0},{13,1},{14,2},{15,3},{28,16},{29,17},{30,18},{31,19},{44,32... | collective-permute-start | bytes 294920 | tf_op jit(solution)/shard_map/while/body/eval_jaxpr/ppermute | solution.py:11
  395.6 10.6 %collective-permute-start.6 = (bf16[64,768]{1,0:T(8,128)(2,1)S(1)}, bf16[64,768]{1,0:T(8,128)(2,1)S(1)}, u32[]{:S(2)}, u32[]{:S(2)}) collective-permute-start(bf16[64,768]{1,0:T(8,128)(2,1)S(1)} %get-tuple-element.1725), channel_id=1, source_target_pairs={{1,0},{2,1},{3,2},{4,3},{5,4},{6,5},{7,6},{8,7},{9,8},{10,9},{11,1... | collective-permute-start | bytes 294920 | tf_op jit(solution)/shard_map/while/body/eval_jaxpr/ppermute | solution.py:11
  411.4 10.6 %collective-permute-start.6 = (bf16[64,768]{1,0:T(8,128)(2,1)S(1)}, bf16[64,768]{1,0:T(8,128)(2,1)S(1)}, u32[]{:S(2)}, u32[]{:S(2)}) collective-permute-start(bf16[64,768]{1,0:T(8,128)(2,1)S(1)} %get-tuple-element.1725), channel_id=1, source_target_pairs={{1,0},{2,1},{3,2},{4,3},{5,4},{6,5},{7,6},{8,7},{9,8},{10,9},{11,1... | collective-permute-start | bytes 294920 | tf_op jit(solution)/shard_map/while/body/eval_jaxpr/ppermute | solution.py:11
  427.2 11.2 %collective-permute-start.6 = (bf16[64,768]{1,0:T(8,128)(2,1)S(1)}, bf16[64,768]{1,0:T(8,128)(2,1)S(1)}, u32[]{:S(2)}, u32[]{:S(2)}) collective-permute-start(bf16[64,768]{1,0:T(8,128)(2,1)S(1)} %get-tuple-element.1725), channel_id=1, source_target_pairs={{1,0},{2,1},{3,2},{4,3},{5,4},{6,5},{7,6},{8,7},{9,8},{10,9},{11,1... | collective-permute-start | bytes 294920 | tf_op jit(solution)/shard_map/while/body/eval_jaxpr/ppermute | solution.py:11
  429.1 9.2 %collective-permute-start.7 = (bf16[64,768]{1,0:T(8,128)(2,1)S(1)}, bf16[64,768]{1,0:T(8,128)(2,1)S(1)}, u32[]{:S(2)}, u32[]{:S(2)}) collective-permute-start(bf16[64,768]{1,0:T(8,128)(2,1)S(1)} %get-tuple-element.1725), channel_id=1, source_target_pairs={{12,0},{13,1},{14,2},{15,3},{28,16},{29,17},{30,18},{31,19},{44,32... | collective-permute-start | bytes 294920 | tf_op jit(solution)/shard_map/while/body/eval_jaxpr/ppermute | solution.py:11
  438.4 11.4 %collective-permute-start.6 = (bf16[64,768]{1,0:T(8,128)(2,1)S(1)}, bf16[64,768]{1,0:T(8,128)(2,1)S(1)}, u32[]{:S(2)}, u32[]{:S(2)}) collective-permute-start(bf16[64,768]{1,0:T(8,128)(2,1)S(1)} %get-tuple-element.1725), channel_id=1, source_target_pairs={{1,0},{2,1},{3,2},{4,3},{5,4},{6,5},{7,6},{8,7},{9,8},{10,9},{11,1... | collective-permute-start | bytes 294920 | tf_op jit(solution)/shard_map/while/body/eval_jaxpr/ppermute | solution.py:11
  440.4 9.5 %collective-permute-start.7 = (bf16[64,768]{1,0:T(8,128)(2,1)S(1)}, bf16[64,768]{1,0:T(8,128)(2,1)S(1)}, u32[]{:S(2)}, u32[]{:S(2)}) collective-permute-start(bf16[64,768]{1,0:T(8,128)(2,1)S(1)} %get-tuple-element.1725), channel_id=1, source_target_pairs={{12,0},{13,1},{14,2},{15,3},{28,16},{29,17},{30,18},{31,19},{44,32... | collective-permute-start | bytes 294920 | tf_op jit(solution)/shard_map/while/body/eval_jaxpr/ppermute | solution.py:11
  449.9 11.2 %collective-permute-start.6 = (bf16[64,768]{1,0:T(8,128)(2,1)S(1)}, bf16[64,768]{1,0:T(8,128)(2,1)S(1)}, u32[]{:S(2)}, u32[]{:S(2)}) collective-permute-start(bf16[64,768]{1,0:T(8,128)(2,1)S(1)} %get-tuple-element.1725), channel_id=1, source_target_pairs={{1,0},{2,1},{3,2},{4,3},{5,4},{6,5},{7,6},{8,7},{9,8},{10,9},{11,1... | collective-permute-start | bytes 294920 | tf_op jit(solution)/shard_map/while/body/eval_jaxpr/ppermute | solution.py:11
  451.9 9.2 %collective-permute-start.7 = (bf16[64,768]{1,0:T(8,128)(2,1)S(1)}, bf16[64,768]{1,0:T(8,128)(2,1)S(1)}, u32[]{:S(2)}, u32[]{:S(2)}) collective-permute-start(bf16[64,768]{1,0:T(8,128)(2,1)S(1)} %get-tuple-element.1725), channel_id=1, source_target_pairs={{12,0},{13,1},{14,2},{15,3},{28,16},{29,17},{30,18},{31,19},{44,32... | collective-permute-start | bytes 294920 | tf_op jit(solution)/shard_map/while/body/eval_jaxpr/ppermute | solution.py:11
  (11 other events, 54.0 us)
Sparse Core Ops, SparseCore 0:
  462.7 162.4 all-reduce.11
where the time goes:
time: 638 us; the launch traced here: 635 us
  waiting for transfers between devices  344 us (54%)
  starting transfers between devices  219 us (34%)
  other arithmetic  20.1 us (3%)
  matrix products  18.7 us (3%)
  local copies, waits for them, and re-layouts  16.1 us (3%)
  between operations  13.5 us (2%)
    ppermute x72, starting transfers between devices, passed_along(): return lax.ppermute(block, axis, route)  219 us
    ppermute x72, waiting for transfers between devices, passed_along(): return lax.ppermute(block, axis, route)  181 us
    psum x1, waiting for transfers between devices, shards(): total = lax.psum(back_state[3], 'dp')  163 us
  transfers between devices with their start and end apart: 73, of which 41 were waited for; matrix products, arithmetic and copies ran while one was open for 1% of the time, Pallas kernels for 0%

commit v1 on v0

--- a/solution.py
+++ b/solution.py
@@ -147,7 +147,9 @@
     back_state = (zero_rows, zero_buffer, zero_buffer, jnp.zeros((channels, channels), jnp.float32))
     back_state = lax.fori_loop(0, split_step, backward_step, back_state)
     back_state = lax.fori_loop(split_step, steps_total, backward_step, back_state)
-    total = lax.psum(back_state[3], "dp")
+    total = back_state[3]
+    for hop in (1, 2, 4, 8, 16):
+        total = total + lax.ppermute(total, "dp", [(dev, dev ^ hop) for dev in range(32)])
     factor = 1.0 / math.sqrt(lax.axis_size("dp") * micro_count * row_count)
     return (total * factor)[None]
 

time: 638 us -> 788 us (1.24)
  the two profiles are of different devices: /device:TPU:64 before, /device:TPU:390 now
where the time goes in v1:
time: 788 us; the launch traced here: 786 us
  waiting for transfers between devices  508 us (64%)
  starting transfers between devices  221 us (28%)
  other arithmetic  19.6 us (2%)
  matrix products  18.7 us (2%)
  local copies, waits for them, and re-layouts  14.7 us (2%)
    ppermute x5, waiting for transfers between devices, shards(): lax.ppermute(total, 'dp', [(dev, dev ^ hop) for dev in range(32)])  356 us
    ppermute x72, starting transfers between devices, passed_along(): return lax.ppermute(block, axis, route)  199 us
    ppermute x72, waiting for transfers between devices, passed_along(): return lax.ppermute(block, axis, route)  152 us
    ppermute x5, starting transfers between devices, shards(): lax.ppermute(total, 'dp', [(dev, dev ^ hop) for dev in range(32)])  21.8 us
  transfers between devices with their start and end apart: 77, of which 61 were waited for; matrix products, arithmetic and copies ran while one was open for 1% of the time, Pallas kernels for 0%

profile of v1, /device:TPU:390, one launch (start us, length us, event | category | flops | bytes accessed | tf_op | source)
XLA Modules:
  0.0 785.5 jit_solution(16363842639990837705)
XLA Ops:
  0.8 62.5 %while.84 = (s32[]{:T(128)}, bf16[64,768]{1,0:T(8,128)(2,1)S(1)}, bf16[3,64,768]{2,1,0:T(8,128)(2,1)S(1)}, bf16[3,64,768]{2,1,0:T(8,128)(2,1)S(1)}, s32[]{:T(128...) while((s32[]{:T(128)}, bf16[64,768]{1,0:T(8,128)(2,1)S(1)}, ...), condition=%wide.region_4.5_spmd, body=%wide.region_0.4_spmd.sunk | while | flops 89710664 | bytes 4455945 | solution.py:104
  4.8 7.3 collective-permute-done.1
  16.2 6.6 collective-permute-done.1
  26.9 7.2 collective-permute-done.1
  38.2 5.3 collective-permute-done.1
  45.5 4.8 collective-permute-start
  50.5 2.4 collective-permute-done.1
  54.9 4.2 collective-permute-start
  59.2 4.1 collective-permute-done.1
  63.3 145.7 %while.85 = (s32[]{:T(128)}, bf16[64,768]{1,0:T(8,128)(2,1)S(1)}, bf16[3,64,768]{2,1,0:T(8,128)(2,1)S(1)}, bf16[3,64,768]{2,1,0:T(8,128)(2,1)S(1)}, s32[]{:T(128...) while((s32[]{:T(128)}, bf16[64,768]{1,0:T(8,128)(2,1)S(1)}, ...), condition=%wide.region_9.10_spmd, body=%wide.region_5.9_spmd.sunk | while | flops 89710664 | bytes 4455965 | solution.py:105
  65.3 7.3 collective-permute-start.2
  76.0 6.5 collective-permute-start.2
  85.4 7.0 collective-permute-start.2
  95.3 6.7 collective-permute-start.2
  104.8 6.5 collective-permute-start.2
  114.2 6.6 collective-permute-start.2
  121.6 12.3 %collective-permute-done.2 = bf16[64,768]{1,0:T(8,128)(2,1)S(1)} collective-permute-done((bf16[64,768]{1,0:T(8,128)(2,1)S(1)}, bf16[64,768]{1,0:T(8,128)(2,1)S(1)}, u32[]{:S(2)}, u32[]{:S(2)}) %collective-permute-start.2) | collective-permute-done | bytes 98336 | tf_op jit(solution)/shard_map/while/body/eval_jaxpr/ppermute | solution.py:11
  133.8 6.2 conditional.9
  144.2 4.8 collective-permute-done.3
  149.1 6.2 conditional.9
  159.6 4.4 collective-permute-done.3
  164.0 6.2 conditional.9
  174.5 4.4 collective-permute-done.3
  180.9 3.3 collective-permute-start.2
  184.3 5.1 collective-permute-done.3
  193.6 5.7 collective-permute-done.3
  203.4 5.6 collective-permute-done.3
  209.7 68.1 %while.86 = (s32[]{:T(128)}, bf16[64,768]{1,0:T(8,128)(2,1)S(1)}, bf16[3,64,768]{2,1,0:T(8,128)(2,1)S(1)}, f32[768,768]{1,0:T(8,128)S(1)}, s32[]{:T(128)}, /*ind...) while((s32[]{:T(128)}, bf16[64,768]{1,0:T(8,128)(2,1)S(1)}, ...), condition=%wide.region_15.16_spmd, body=%wide.region_10.15_spmd.sunk | while | flops 155271552 | bytes 11747327 | solution.py:148
  213.7 4.8 collective-permute-done.4
  222.5 4.2 collective-permute-done.4
  226.7 2.2 collective-permute-start.5
  231.2 11.2 %collective-permute-done.4 = bf16[64,768]{1,0:T(8,128)(2,1)S(1)} collective-permute-done((bf16[64,768]{1,0:T(8,128)(2,1)S(1)}, bf16[64,768]{1,0:T(8,128)(2,1)S(1)}, u32[]{:S(2)}, u32[]{:S(2)}) %collective-permute-start.4) | collective-permute-done | bytes 98336 | tf_op jit(solution)/shard_map/while/body/eval_jaxpr/ppermute | solution.py:11
  242.4 5.1 conditional.10
  251.1 3.7 collective-permute-done.4
  254.8 5.1 conditional.10
  263.5 3.7 collective-permute-done.4
  267.2 5.1 conditional.10
  277.8 126.9 %while.87 = (s32[]{:T(128)}, bf16[64,768]{1,0:T(8,128)(2,1)S(1)}, bf16[3,64,768]{2,1,0:T(8,128)(2,1)S(1)}, f32[768,768]{1,0:T(8,128)S(1)}, s32[]{:T(128)}, /*ind...) while((s32[]{:T(128)}, bf16[64,768]{1,0:T(8,128)(2,1)S(1)}, ...), condition=%wide.region_21.22_spmd, body=%wide.region_16.21_spmd.sunk | while | flops 155271552 | bytes 11747347 | solution.py:149
  277.8 4.7 collective-permute-start.7
  282.5 4.9 collective-permute-start.6
  291.3 2.7 collective-permute-start.6
  296.2 3.8 collective-permute-start.7
  304.2 4.6 collective-permute-start.7
  312.9 4.6 collective-permute-start.7
  321.6 4.6 collective-permute-start.7
  330.4 4.6 collective-permute-start.7
  339.1 4.6 collective-permute-start.7
  347.8 4.6 collective-permute-start.7
  354.6 11.5 %collective-permute-done.6 = bf16[64,768]{1,0:T(8,128)(2,1)S(1)} collective-permute-done((bf16[64,768]{1,0:T(8,128)(2,1)S(1)}, bf16[64,768]{1,0:T(8,128)(2,1)S(1)}, u32[]{:S(2)}, u32[]{:S(2)}) %collective-permute-start.6) | collective-permute-done | bytes 98336 | tf_op jit(solution)/shard_map/while/body/eval_jaxpr/ppermute | solution.py:11
  366.1 6.7 collective-permute-start.7
  375.1 4.9 collective-permute-done.6
  380.0 6.7 collective-permute-start.7
  388.9 4.9 collective-permute-done.6
  393.9 6.7 collective-permute-start.7
  404.7 2.7 collective-permute-start.8
  407.5 52.3 %collective-permute-done.8 = f32[768,768]{1,0:T(8,128)S(1)} collective-permute-done((f32[768,768]{1,0:T(8,128)S(1)}, f32[768,768]{1,0:T(8,128)S(1)}, u32[]{:S(2)}, u32[]{:S(2)}) %collective-permute-start.8) | collective-permute-done | bytes 2359328 | tf_op jit(solution)/shard_map/ppermute | solution.py:152
  460.0 3.3 collective-permute-start.9
  463.4 52.3 %collective-permute-done.9 = f32[768,768]{1,0:T(8,128)S(1)} collective-permute-done((f32[768,768]{1,0:T(8,128)S(1)}, f32[768,768]{1,0:T(8,128)S(1)}, u32[]{:S(2)}, u32[]{:S(2)}) %collective-permute-start.9) | collective-permute-done | bytes 2359328 | tf_op jit(solution)/shard_map/ppermute | solution.py:152
  516.0 3.5 collective-permute-start.10
  519.5 49.7 %collective-permute-done.10 = f32[768,768]{1,0:T(8,128)S(1)} collective-permute-done((f32[768,768]{1,0:T(8,128)S(1)}, f32[768,768]{1,0:T(8,128)S(1)}, u32[]{:S(2)}, u32[]{:S(2)}) %collective-permute-start.10) | collective-permute-done | bytes 2359328 | tf_op jit(solution)/shard_map/ppermute | solution.py:152
  569.5 4.5 collective-permute-start.11
  574.0 99.3 %collective-permute-done.11 = f32[768,768]{1,0:T(8,128)S(1)} collective-permute-done((f32[768,768]{1,0:T(8,128)S(1)}, f32[768,768]{1,0:T(8,128)S(1)}, u32[]{:S(2)}, u32[]{:S(2)}) %collective-permute-start.11) | collective-permute-done | bytes 2359328 | tf_op jit(solution)/shard_map/ppermute | solution.py:152
  673.6 7.7 collective-permute-start.12
  681.3 102.5 %collective-permute-done.12 = f32[768,768]{1,0:T(8,128)S(1)} collective-permute-done((f32[768,768]{1,0:T(8,128)S(1)}, f32[768,768]{1,0:T(8,128)S(1)}, u32[]{:S(2)}, u32[]{:S(2)}) %collective-permute-start.12) | collective-permute-done | bytes 2359328 | tf_op jit(solution)/shard_map/ppermute | solution.py:152
  (342 shorter events, 172.0 us)
Async XLA Ops:
  1.5 10.6 %collective-permute-start.1 = (bf16[64,768]{1,0:T(8,128)(2,1)S(1)}, bf16[64,768]{1,0:T(8,128)(2,1)S(1)}, u32[]{:S(2)}, u32[]{:S(2)}) collective-permute-start(bf16[64,768]{1,0:T(8,128)(2,1)S(1)} %get-tuple-element.1675), channel_id=1, source_target_pairs={{0,12},{1,13},{2,14},{3,15},{16,28},{17,29},{18,30},{19,31},{32,44... | collective-permute-start | bytes 294920 | tf_op jit(solution)/shard_map/while/body/eval_jaxpr/ppermute | solution.py:11
  2.8 9.4 %collective-permute-start = (bf16[64,768]{1,0:T(8,128)(2,1)S(1)}, bf16[64,768]{1,0:T(8,128)(2,1)S(1)}, u32[]{:S(2)}, u32[]{:S(2)}) collective-permute-start(bf16[64,768]{1,0:T(8,128)(2,1)S(1)} %get-tuple-element.1675), channel_id=1, source_target_pairs={{0,1},{1,2},{2,3},{3,4},{4,5},{5,6},{6,7},{7,8},{8,9},{9,10},{10,1... | collective-permute-start | bytes 294920 | tf_op jit(solution)/shard_map/while/body/eval_jaxpr/ppermute | solution.py:11
  12.9 9.9 %collective-permute-start.1 = (bf16[64,768]{1,0:T(8,128)(2,1)S(1)}, bf16[64,768]{1,0:T(8,128)(2,1)S(1)}, u32[]{:S(2)}, u32[]{:S(2)}) collective-permute-start(bf16[64,768]{1,0:T(8,128)(2,1)S(1)} %get-tuple-element.1675), channel_id=1, source_target_pairs={{0,12},{1,13},{2,14},{3,15},{16,28},{17,29},{18,30},{19,31},{32,44... | collective-permute-start | bytes 294920 | tf_op jit(solution)/shard_map/while/body/eval_jaxpr/ppermute | solution.py:11
  14.1 8.6 %collective-permute-start = (bf16[64,768]{1,0:T(8,128)(2,1)S(1)}, bf16[64,768]{1,0:T(8,128)(2,1)S(1)}, u32[]{:S(2)}, u32[]{:S(2)}) collective-permute-start(bf16[64,768]{1,0:T(8,128)(2,1)S(1)} %get-tuple-element.1675), channel_id=1, source_target_pairs={{0,1},{1,2},{2,3},{3,4},{4,5},{5,6},{6,7},{7,8},{8,9},{9,10},{10,1... | collective-permute-start | bytes 294920 | tf_op jit(solution)/shard_map/while/body/eval_jaxpr/ppermute | solution.py:11
  23.5 10.7 %collective-permute-start.1 = (bf16[64,768]{1,0:T(8,128)(2,1)S(1)}, bf16[64,768]{1,0:T(8,128)(2,1)S(1)}, u32[]{:S(2)}, u32[]{:S(2)}) collective-permute-start(bf16[64,768]{1,0:T(8,128)(2,1)S(1)} %get-tuple-element.1675), channel_id=1, source_target_pairs={{0,12},{1,13},{2,14},{3,15},{16,28},{17,29},{18,30},{19,31},{32,44... | collective-permute-start | bytes 294920 | tf_op jit(solution)/shard_map/while/body/eval_jaxpr/ppermute | solution.py:11
  24.8 9.4 %collective-permute-start = (bf16[64,768]{1,0:T(8,128)(2,1)S(1)}, bf16[64,768]{1,0:T(8,128)(2,1)S(1)}, u32[]{:S(2)}, u32[]{:S(2)}) collective-permute-start(bf16[64,768]{1,0:T(8,128)(2,1)S(1)} %get-tuple-element.1675), channel_id=1, source_target_pairs={{0,1},{1,2},{2,3},{3,4},{4,5},{5,6},{6,7},{7,8},{8,9},{9,10},{10,1... | collective-permute-start | bytes 294920 | tf_op jit(solution)/shard_map/while/body/eval_jaxpr/ppermute | solution.py:11
  34.9 8.6 %collective-permute-start.1 = (bf16[64,768]{1,0:T(8,128)(2,1)S(1)}, bf16[64,768]{1,0:T(8,128)(2,1)S(1)}, u32[]{:S(2)}, u32[]{:S(2)}) collective-permute-start(bf16[64,768]{1,0:T(8,128)(2,1)S(1)} %get-tuple-element.1675), channel_id=1, source_target_pairs={{0,12},{1,13},{2,14},{3,15},{16,28},{17,29},{18,30},{19,31},{32,44... | collective-permute-start | bytes 294920 | tf_op jit(solution)/shard_map/while/body/eval_jaxpr/ppermute | solution.py:11
  36.2 7.4 collective-permute-start
  44.3 8.6 %collective-permute-start.1 = (bf16[64,768]{1,0:T(8,128)(2,1)S(1)}, bf16[64,768]{1,0:T(8,128)(2,1)S(1)}, u32[]{:S(2)}, u32[]{:S(2)}) collective-permute-start(bf16[64,768]{1,0:T(8,128)(2,1)S(1)} %get-tuple-element.1675), channel_id=1, source_target_pairs={{0,12},{1,13},{2,14},{3,15},{16,28},{17,29},{18,30},{19,31},{32,44... | collective-permute-start | bytes 294920 | tf_op jit(solution)/shard_map/while/body/eval_jaxpr/ppermute | solution.py:11
  45.5 7.4 collective-permute-start
  53.6 9.7 %collective-permute-start.1 = (bf16[64,768]{1,0:T(8,128)(2,1)S(1)}, bf16[64,768]{1,0:T(8,128)(2,1)S(1)}, u32[]{:S(2)}, u32[]{:S(2)}) collective-permute-start(bf16[64,768]{1,0:T(8,128)(2,1)S(1)} %get-tuple-element.1675), channel_id=1, source_target_pairs={{0,12},{1,13},{2,14},{3,15},{16,28},{17,29},{18,30},{19,31},{32,44... | collective-permute-start | bytes 294920 | tf_op jit(solution)/shard_map/while/body/eval_jaxpr/ppermute | solution.py:11
  54.9 8.4 %collective-permute-start = (bf16[64,768]{1,0:T(8,128)(2,1)S(1)}, bf16[64,768]{1,0:T(8,128)(2,1)S(1)}, u32[]{:S(2)}, u32[]{:S(2)}) collective-permute-start(bf16[64,768]{1,0:T(8,128)(2,1)S(1)} %get-tuple-element.1675), channel_id=1, source_target_pairs={{0,1},{1,2},{2,3},{3,4},{4,5},{5,6},{6,7},{7,8},{8,9},{9,10},{10,1... | collective-permute-start | bytes 294920 | tf_op jit(solution)/shard_map/while/body/eval_jaxpr/ppermute | solution.py:11
  64.0 10.0 %collective-permute-start.3 = (bf16[64,768]{1,0:T(8,128)(2,1)S(1)}, bf16[64,768]{1,0:T(8,128)(2,1)S(1)}, u32[]{:S(2)}, u32[]{:S(2)}) collective-permute-start(bf16[64,768]{1,0:T(8,128)(2,1)S(1)} %get-tuple-element.1691), channel_id=1, source_target_pairs={{0,12},{1,13},{2,14},{3,15},{16,28},{17,29},{18,30},{19,31},{32,44... | collective-permute-start | bytes 294920 | tf_op jit(solution)/shard_map/while/body/eval_jaxpr/ppermute | solution.py:11
  65.3 8.7 %collective-permute-start.2 = (bf16[64,768]{1,0:T(8,128)(2,1)S(1)}, bf16[64,768]{1,0:T(8,128)(2,1)S(1)}, u32[]{:S(2)}, u32[]{:S(2)}) collective-permute-start(bf16[64,768]{1,0:T(8,128)(2,1)S(1)} %get-tuple-element.1691), channel_id=1, source_target_pairs={{0,1},{1,2},{2,3},{3,4},{4,5},{5,6},{6,7},{7,8},{8,9},{9,10},{10,1... | collective-permute-start | bytes 294920 | tf_op jit(solution)/shard_map/while/body/eval_jaxpr/ppermute | solution.py:11
  74.7 8.6 %collective-permute-start.3 = (bf16[64,768]{1,0:T(8,128)(2,1)S(1)}, bf16[64,768]{1,0:T(8,128)(2,1)S(1)}, u32[]{:S(2)}, u32[]{:S(2)}) collective-permute-start(bf16[64,768]{1,0:T(8,128)(2,1)S(1)} %get-tuple-element.1691), channel_id=1, source_target_pairs={{0,12},{1,13},{2,14},{3,15},{16,28},{17,29},{18,30},{19,31},{32,44... | collective-permute-start | bytes 294920 | tf_op jit(solution)/shard_map/while/body/eval_jaxpr/ppermute | solution.py:11
  76.0 7.4 collective-permute-start.2
  84.1 8.8 %collective-permute-start.3 = (bf16[64,768]{1,0:T(8,128)(2,1)S(1)}, bf16[64,768]{1,0:T(8,128)(2,1)S(1)}, u32[]{:S(2)}, u32[]{:S(2)}) collective-permute-start(bf16[64,768]{1,0:T(8,128)(2,1)S(1)} %get-tuple-element.1691), channel_id=1, source_target_pairs={{0,12},{1,13},{2,14},{3,15},{16,28},{17,29},{18,30},{19,31},{32,44... | collective-permute-start | bytes 294920 | tf_op jit(solution)/shard_map/while/body/eval_jaxpr/ppermute | solution.py:11
  85.4 7.9 %collective-permute-start.2 = (bf16[64,768]{1,0:T(8,128)(2,1)S(1)}, bf16[64,768]{1,0:T(8,128)(2,1)S(1)}, u32[]{:S(2)}, u32[]{:S(2)}) collective-permute-start(bf16[64,768]{1,0:T(8,128)(2,1)S(1)} %get-tuple-element.1691), channel_id=1, source_target_pairs={{0,1},{1,2},{2,3},{3,4},{4,5},{5,6},{6,7},{7,8},{8,9},{9,10},{10,1... | collective-permute-start | bytes 294920 | tf_op jit(solution)/shard_map/while/body/eval_jaxpr/ppermute | solution.py:11
  94.0 8.6 %collective-permute-start.3 = (bf16[64,768]{1,0:T(8,128)(2,1)S(1)}, bf16[64,768]{1,0:T(8,128)(2,1)S(1)}, u32[]{:S(2)}, u32[]{:S(2)}) collective-permute-start(bf16[64,768]{1,0:T(8,128)(2,1)S(1)} %get-tuple-element.1691), channel_id=1, source_target_pairs={{0,12},{1,13},{2,14},{3,15},{16,28},{17,29},{18,30},{19,31},{32,44... | collective-permute-start | bytes 294920 | tf_op jit(solution)/shard_map/while/body/eval_jaxpr/ppermute | solution.py:11
  95.3 7.6 collective-permute-start.2
  103.6 8.6 %collective-permute-start.3 = (bf16[64,768]{1,0:T(8,128)(2,1)S(1)}, bf16[64,768]{1,0:T(8,128)(2,1)S(1)}, u32[]{:S(2)}, u32[]{:S(2)}) collective-permute-start(bf16[64,768]{1,0:T(8,128)(2,1)S(1)} %get-tuple-element.1691), channel_id=1, source_target_pairs={{0,12},{1,13},{2,14},{3,15},{16,28},{17,29},{18,30},{19,31},{32,44... | collective-permute-start | bytes 294920 | tf_op jit(solution)/shard_map/while/body/eval_jaxpr/ppermute | solution.py:11
  104.8 7.4 collective-permute-start.2
  112.9 8.6 %collective-permute-start.3 = (bf16[64,768]{1,0:T(8,128)(2,1)S(1)}, bf16[64,768]{1,0:T(8,128)(2,1)S(1)}, u32[]{:S(2)}, u32[]{:S(2)}) collective-permute-start(bf16[64,768]{1,0:T(8,128)(2,1)S(1)} %get-tuple-element.1691), channel_id=1, source_target_pairs={{0,12},{1,13},{2,14},{3,15},{16,28},{17,29},{18,30},{19,31},{32,44... | collective-permute-start | bytes 294920 | tf_op jit(solution)/shard_map/while/body/eval_jaxpr/ppermute | solution.py:11
  114.2 19.6 %collective-permute-start.2 = (bf16[64,768]{1,0:T(8,128)(2,1)S(1)}, bf16[64,768]{1,0:T(8,128)(2,1)S(1)}, u32[]{:S(2)}, u32[]{:S(2)}) collective-permute-start(bf16[64,768]{1,0:T(8,128)(2,1)S(1)} %get-tuple-element.1691), channel_id=1, source_target_pairs={{0,1},{1,2},{2,3},{3,4},{4,5},{5,6},{6,7},{7,8},{8,9},{9,10},{10,1... | collective-permute-start | bytes 294920 | tf_op jit(solution)/shard_map/while/body/eval_jaxpr/ppermute | solution.py:11
  140.0 9.0 %collective-permute-start.3 = (bf16[64,768]{1,0:T(8,128)(2,1)S(1)}, bf16[64,768]{1,0:T(8,128)(2,1)S(1)}, u32[]{:S(2)}, u32[]{:S(2)}) collective-permute-start(bf16[64,768]{1,0:T(8,128)(2,1)S(1)} %get-tuple-element.1691), channel_id=1, source_target_pairs={{0,12},{1,13},{2,14},{3,15},{16,28},{17,29},{18,30},{19,31},{32,44... | collective-permute-start | bytes 294920 | tf_op jit(solution)/shard_map/while/body/eval_jaxpr/ppermute | solution.py:11
  141.3 7.7 collective-permute-start.2
  155.4 8.6 %collective-permute-start.3 = (bf16[64,768]{1,0:T(8,128)(2,1)S(1)}, bf16[64,768]{1,0:T(8,128)(2,1)S(1)}, u32[]{:S(2)}, u32[]{:S(2)}) collective-permute-start(bf16[64,768]{1,0:T(8,128)(2,1)S(1)} %get-tuple-element.1691), channel_id=1, source_target_pairs={{0,12},{1,13},{2,14},{3,15},{16,28},{17,29},{18,30},{19,31},{32,44... | collective-permute-start | bytes 294920 | tf_op jit(solution)/shard_map/while/body/eval_jaxpr/ppermute | solution.py:11
  156.7 7.4 collective-permute-start.2
  170.3 8.6 %collective-permute-start.3 = (bf16[64,768]{1,0:T(8,128)(2,1)S(1)}, bf16[64,768]{1,0:T(8,128)(2,1)S(1)}, u32[]{:S(2)}, u32[]{:S(2)}) collective-permute-start(bf16[64,768]{1,0:T(8,128)(2,1)S(1)} %get-tuple-element.1691), channel_id=1, source_target_pairs={{0,12},{1,13},{2,14},{3,15},{16,28},{17,29},{18,30},{19,31},{32,44... | collective-permute-start | bytes 294920 | tf_op jit(solution)/shard_map/while/body/eval_jaxpr/ppermute | solution.py:11
  171.6 7.4 collective-permute-start.2
  179.7 9.8 %collective-permute-start.3 = (bf16[64,768]{1,0:T(8,128)(2,1)S(1)}, bf16[64,768]{1,0:T(8,128)(2,1)S(1)}, u32[]{:S(2)}, u32[]{:S(2)}) collective-permute-start(bf16[64,768]{1,0:T(8,128)(2,1)S(1)} %get-tuple-element.1691), channel_id=1, source_target_pairs={{0,12},{1,13},{2,14},{3,15},{16,28},{17,29},{18,30},{19,31},{32,44... | collective-permute-start | bytes 294920 | tf_op jit(solution)/shard_map/while/body/eval_jaxpr/ppermute | solution.py:11
  180.9 8.6 %collective-permute-start.2 = (bf16[64,768]{1,0:T(8,128)(2,1)S(1)}, bf16[64,768]{1,0:T(8,128)(2,1)S(1)}, u32[]{:S(2)}, u32[]{:S(2)}) collective-permute-start(bf16[64,768]{1,0:T(8,128)(2,1)S(1)} %get-tuple-element.1691), channel_id=1, source_target_pairs={{0,1},{1,2},{2,3},{3,4},{4,5},{5,6},{6,7},{7,8},{8,9},{9,10},{10,1... | collective-permute-start | bytes 294920 | tf_op jit(solution)/shard_map/while/body/eval_jaxpr/ppermute | solution.py:11
  190.2 9.1 %collective-permute-start.3 = (bf16[64,768]{1,0:T(8,128)(2,1)S(1)}, bf16[64,768]{1,0:T(8,128)(2,1)S(1)}, u32[]{:S(2)}, u32[]{:S(2)}) collective-permute-start(bf16[64,768]{1,0:T(8,128)(2,1)S(1)} %get-tuple-element.1691), channel_id=1, source_target_pairs={{0,12},{1,13},{2,14},{3,15},{16,28},{17,29},{18,30},{19,31},{32,44... | collective-permute-start | bytes 294920 | tf_op jit(solution)/shard_map/while/body/eval_jaxpr/ppermute | solution.py:11
  191.5 7.9 %collective-permute-start.2 = (bf16[64,768]{1,0:T(8,128)(2,1)S(1)}, bf16[64,768]{1,0:T(8,128)(2,1)S(1)}, u32[]{:S(2)}, u32[]{:S(2)}) collective-permute-start(bf16[64,768]{1,0:T(8,128)(2,1)S(1)} %get-tuple-element.1691), channel_id=1, source_target_pairs={{0,1},{1,2},{2,3},{3,4},{4,5},{5,6},{6,7},{7,8},{8,9},{9,10},{10,1... | collective-permute-start | bytes 294920 | tf_op jit(solution)/shard_map/while/body/eval_jaxpr/ppermute | solution.py:11
  200.1 8.9 %collective-permute-start.3 = (bf16[64,768]{1,0:T(8,128)(2,1)S(1)}, bf16[64,768]{1,0:T(8,128)(2,1)S(1)}, u32[]{:S(2)}, u32[]{:S(2)}) collective-permute-start(bf16[64,768]{1,0:T(8,128)(2,1)S(1)} %get-tuple-element.1691), channel_id=1, source_target_pairs={{0,12},{1,13},{2,14},{3,15},{16,28},{17,29},{18,30},{19,31},{32,44... | collective-permute-start | bytes 294920 | tf_op jit(solution)/shard_map/while/body/eval_jaxpr/ppermute | solution.py:11
  201.4 7.6 collective-permute-start.2
  211.5 7.0 collective-permute-start.4
  220.2 6.5 collective-permute-start.4
  226.7 4.4 collective-permute-start.5
  229.0 13.5 %collective-permute-start.4 = (bf16[64,768]{1,0:T(8,128)(2,1)S(1)}, bf16[64,768]{1,0:T(8,128)(2,1)S(1)}, u32[]{:S(2)}, u32[]{:S(2)}) collective-permute-start(bf16[64,768]{1,0:T(8,128)(2,1)S(1)} %get-tuple-element.1709), channel_id=1, source_target_pairs={{1,0},{2,1},{3,2},{4,3},{5,4},{6,5},{7,6},{8,7},{9,8},{10,9},{11,1... | collective-permute-start | bytes 294920 | tf_op jit(solution)/shard_map/while/body/eval_jaxpr/ppermute | solution.py:11
  248.9 5.9 collective-permute-start.4
  261.3 5.9 collective-permute-start.4
  277.8 9.6 %collective-permute-start.7 = (bf16[64,768]{1,0:T(8,128)(2,1)S(1)}, bf16[64,768]{1,0:T(8,128)(2,1)S(1)}, u32[]{:S(2)}, u32[]{:S(2)}) collective-permute-start(bf16[64,768]{1,0:T(8,128)(2,1)S(1)} %get-tuple-element.1725), channel_id=1, source_target_pairs={{12,0},{13,1},{14,2},{15,3},{28,16},{29,17},{30,18},{31,19},{44,32... | collective-permute-start | bytes 294920 | tf_op jit(solution)/shard_map/while/body/eval_jaxpr/ppermute | solution.py:11
  282.5 7.1 collective-permute-start.6
  289.6 4.5 collective-permute-start.7
  291.3 4.9 collective-permute-start.6
  296.2 6.0 collective-permute-start.7
  304.2 6.8 collective-permute-start.7
  312.9 6.8 collective-permute-start.7
  321.6 6.8 collective-permute-start.7
  330.4 6.8 collective-permute-start.7
  339.1 6.8 collective-permute-start.7
  347.8 6.8 collective-permute-start.7
  352.4 13.7 %collective-permute-start.6 = (bf16[64,768]{1,0:T(8,128)(2,1)S(1)}, bf16[64,768]{1,0:T(8,128)(2,1)S(1)}, u32[]{:S(2)}, u32[]{:S(2)}) collective-permute-start(bf16[64,768]{1,0:T(8,128)(2,1)S(1)} %get-tuple-element.1725), channel_id=1, source_target_pairs={{1,0},{2,1},{3,2},{4,3},{5,4},{6,5},{7,6},{8,7},{9,8},{10,9},{11,1... | collective-permute-start | bytes 294920 | tf_op jit(solution)/shard_map/while/body/eval_jaxpr/ppermute | solution.py:11
  366.1 8.9 %collective-permute-start.7 = (bf16[64,768]{1,0:T(8,128)(2,1)S(1)}, bf16[64,768]{1,0:T(8,128)(2,1)S(1)}, u32[]{:S(2)}, u32[]{:S(2)}) collective-permute-start(bf16[64,768]{1,0:T(8,128)(2,1)S(1)} %get-tuple-element.1725), channel_id=1, source_target_pairs={{12,0},{13,1},{14,2},{15,3},{28,16},{29,17},{30,18},{31,19},{44,32... | collective-permute-start | bytes 294920 | tf_op jit(solution)/shard_map/while/body/eval_jaxpr/ppermute | solution.py:11
  372.8 7.2 collective-permute-start.6
  380.0 8.9 %collective-permute-start.7 = (bf16[64,768]{1,0:T(8,128)(2,1)S(1)}, bf16[64,768]{1,0:T(8,128)(2,1)S(1)}, u32[]{:S(2)}, u32[]{:S(2)}) collective-permute-start(bf16[64,768]{1,0:T(8,128)(2,1)S(1)} %get-tuple-element.1725), channel_id=1, source_target_pairs={{12,0},{13,1},{14,2},{15,3},{28,16},{29,17},{30,18},{31,19},{44,32... | collective-permute-start | bytes 294920 | tf_op jit(solution)/shard_map/while/body/eval_jaxpr/ppermute | solution.py:11
  386.7 7.1 collective-permute-start.6
  393.9 8.9 %collective-permute-start.7 = (bf16[64,768]{1,0:T(8,128)(2,1)S(1)}, bf16[64,768]{1,0:T(8,128)(2,1)S(1)}, u32[]{:S(2)}, u32[]{:S(2)}) collective-permute-start(bf16[64,768]{1,0:T(8,128)(2,1)S(1)} %get-tuple-element.1725), channel_id=1, source_target_pairs={{12,0},{13,1},{14,2},{15,3},{28,16},{29,17},{30,18},{31,19},{44,32... | collective-permute-start | bytes 294920 | tf_op jit(solution)/shard_map/while/body/eval_jaxpr/ppermute | solution.py:11
  404.7 55.0 %collective-permute-start.8 = (f32[768,768]{1,0:T(8,128)S(1)}, f32[768,768]{1,0:T(8,128)S(1)}, u32[]{:S(2)}, u32[]{:S(2)}) collective-permute-start(f32[768,768]{1,0:T(8,128)S(1)} %get-tuple-element.1220), channel_id=1, source_target_pairs={{0,16},{16,0},{32,48},{48,32},{64,80},{80,64},{96,112},{112,96},{1... | collective-permute-start | bytes 7077896 | tf_op jit(solution)/shard_map/ppermute | solution.py:152
  460.0 55.7 %collective-permute-start.9 = (f32[768,768]{1,0:T(8,128)S(1)}, f32[768,768]{1,0:T(8,128)S(1)}, u32[]{:S(2)}, u32[]{:S(2)}) collective-permute-start(f32[768,768]{1,0:T(8,128)S(1)} %add.333), channel_id=1, source_target_pairs={{0,32},{16,48},{32,0},{48,16},{64,96},{80,112},{96,64},{112,80},{1... | collective-permute-start | bytes 7077896 | tf_op jit(solution)/shard_map/ppermute | solution.py:152
  516.0 53.2 %collective-permute-start.10 = (f32[768,768]{1,0:T(8,128)S(1)}, f32[768,768]{1,0:T(8,128)S(1)}, u32[]{:S(2)}, u32[]{:S(2)}) collective-permute-start(f32[768,768]{1,0:T(8,128)S(1)} %add.334), channel_id=1, source_target_pairs={{0,64},{16,80},{32,96},{48,112},{64,0},{80,16},{96,32},{112,48},{1... | collective-permute-start | bytes 7077896 | tf_op jit(solution)/shard_map/ppermute | solution.py:152
  569.5 103.8 %collective-permute-start.11 = (f32[768,768]{1,0:T(8,128)S(1)}, f32[768,768]{1,0:T(8,128)S(1)}, u32[]{:S(2)}, u32[]{:S(2)}) collective-permute-start(f32[768,768]{1,0:T(8,128)S(1)} %add.335), channel_id=1, source_target_pairs={{0,128},{16,144},{32,160},{48,176},{64,192},{80,208},{96,224},{112... | collective-permute-start | bytes 7077896 | tf_op jit(solution)/shard_map/ppermute | solution.py:152
  673.6 110.2 %collective-permute-start.12 = (f32[768,768]{1,0:T(8,128)S(1)}, f32[768,768]{1,0:T(8,128)S(1)}, u32[]{:S(2)}, u32[]{:S(2)}) collective-permute-start(f32[768,768]{1,0:T(8,128)S(1)} %add.336), channel_id=1, source_target_pairs={{0,256},{16,272},{32,288},{48,304},{64,320},{80,336},{96,352},{112... | collective-permute-start | bytes 7077896 | tf_op jit(solution)/shard_map/ppermute | solution.py:152
  (14 other events, 52.0 us)
